TPU v7x, 32 devices: a whole 2x2x4 slice. The times are simulated.
32 devices in a mesh: tm: 4 (over x, core), patch: 8 (over z, y).
Axes of the slice: x: 2, y: 2, z: 4, core: 2. Of those that a mesh axis runs over, the one named last changes fastest.
Arguments:
- stream: bfloat16 [4, 448, 1152], P('tm', 'patch'), may hold values from -6 to 6
- stale_keys: bfloat16 [4, 448, 1152], P(None, 'patch', 'tm'), may hold values from -10 to 10
- stale_values: bfloat16 [4, 448, 1152], P(None, 'patch', 'tm'), may hold values from -6 to 6
- modulation: float32 [2, 3, 1152], replicated, may hold values from -4 to 4
- w_qkv: bfloat16 [2, 3, 1152, 1152], P(None, None, 'tm'), may hold values from -0.1875 to 0.1875
- w_out: bfloat16 [2, 1152, 1152], P(None, 'tm'), may hold values from -0.1875 to 0.1875
- qk_gain: float32 [2, 2, 72], replicated, may hold values from 1.4 to 7
Outputs:
- output: bfloat16 [4, 448, 1152], P('tm', 'patch')
All inputs are finite; a program needn't handle non-finite values.
Results may differ from a plain program's by a relative error of at most 0.035.
Values may be sent and summed in bfloat16 or wider, within the bound.
A program may use at most 64 MiB of HBM per device.

v0:
```python
import jax
import jax.numpy as jnp
from jax import lax
from jax.sharding import PartitionSpec as P

HEAD_DIM = 72


EPS = 1e-06


def softmax_rows(scores):
    top = jnp.max(scores, axis=-1, keepdims=True)
    expo = jnp.exp(scores - top)
    return expo / jnp.sum(expo, axis=-1, keepdims=True)


def modulate(stream, shift, scale):
    values = stream.astype(jnp.float32)
    center = jnp.mean(values, axis=-1, keepdims=True)
    spread = jnp.mean(jnp.square(values - center), axis=-1, keepdims=True)
    normed = (values - center) * lax.rsqrt(spread + EPS)
    return (normed * (1.0 + scale) + shift).astype(jnp.bfloat16)


def head_norm(values, gain):
    factor = lax.rsqrt(jnp.mean(values * values, axis=-1, keepdims=True) + EPS)
    return (values * factor * gain).astype(jnp.bfloat16)


def projections(hmod, weights, gains):
    mixed = jnp.einsum("fpd,ced->cfpe", hmod, weights, preferred_element_type=jnp.float32)
    width = mixed.shape[3]
    shaped = mixed.reshape(3, mixed.shape[1], mixed.shape[2], width // HEAD_DIM, HEAD_DIM)
    query = head_norm(shaped[0], gains[0])
    keys = head_norm(shaped[1], gains[1])
    values = shaped[2].astype(jnp.bfloat16)
    return jnp.stack([query, keys, values]).reshape(mixed.shape)


def front_end(modulation, w_qkv, qk_gain, block, piece):
    hmod = modulate(piece, modulation[block, 0], modulation[block, 1])
    return projections(hmod, w_qkv[block], qk_gain[block])


def local(stream, stale_keys, stale_values, modulation, w_qkv, w_out, qk_gain):
    rows = stream.shape[1]
    local_width = w_out.shape[1]
    heads_here = local_width // HEAD_DIM
    factor = HEAD_DIM ** (-0.5)
    packed = front_end(
        modulation, w_qkv, qk_gain, 0, lax.all_gather(stream, "tm", axis=0, tiled=True)
    )
    frames = packed.shape[1]
    old_keys, old_values = (
        lax.all_gather(stale_keys, "patch", axis=1, tiled=True),
        lax.all_gather(stale_values, "patch", axis=1, tiled=True),
    )
    spatial_len = old_keys.shape[1]
    offset = lax.axis_index("patch") * rows
    keys = lax.dynamic_update_slice_in_dim(old_keys, packed[1], offset, 1)
    values = lax.dynamic_update_slice_in_dim(old_values, packed[2], offset, 1)
    query4 = packed[0].reshape(frames, rows, heads_here, HEAD_DIM)
    keys4 = keys.reshape(frames, spatial_len, heads_here, HEAD_DIM)
    values4 = values.reshape(frames, spatial_len, heads_here, HEAD_DIM)
    scores = (
        jnp.einsum("fqhd,fkhd->fhqk", query4, keys4, preferred_element_type=jnp.float32) * factor
    )
    weights = softmax_rows(scores).astype(jnp.bfloat16)
    attn = jnp.einsum("fhqk,fkhd->fqhd", weights, values4, preferred_element_type=jnp.float32)
    attn = attn.astype(jnp.bfloat16).reshape(frames, rows, local_width)
    partial_mid = jnp.einsum("fpe,ed->fpd", attn, w_out[0], preferred_element_type=jnp.float32)
    summed = lax.psum_scatter(
        partial_mid.astype(jnp.bfloat16), "tm", scatter_dimension=0, tiled=True
    ).astype(jnp.float32)
    middle = (stream.astype(jnp.float32) + modulation[0, 2] * summed).astype(jnp.bfloat16)
    packed = front_end(
        modulation, w_qkv, qk_gain, 1, lax.all_gather(middle, "tm", axis=0, tiled=True)
    )
    query4 = packed[0].reshape(frames, rows, heads_here, HEAD_DIM)
    keys4 = packed[1].reshape(frames, rows, heads_here, HEAD_DIM)
    values4 = packed[2].reshape(frames, rows, heads_here, HEAD_DIM)
    scores = (
        jnp.einsum("fphd,gphd->phfg", query4, keys4, preferred_element_type=jnp.float32) * factor
    )
    weights = softmax_rows(scores).astype(jnp.bfloat16)
    attn = jnp.einsum("phfg,gphd->fphd", weights, values4, preferred_element_type=jnp.float32)
    attn = attn.astype(jnp.bfloat16).reshape(frames, rows, local_width)
    partial_out = jnp.einsum("fpe,ed->fpd", attn, w_out[1], preferred_element_type=jnp.float32)
    summed_out = lax.psum_scatter(
        partial_out.astype(jnp.bfloat16), "tm", scatter_dimension=0, tiled=True
    ).astype(jnp.float32)
    return (middle.astype(jnp.float32) + modulation[1, 2] * summed_out).astype(jnp.bfloat16)


def solution(mesh):
    placed = (
        P("tm", "patch", None),
        P(None, "patch", "tm"),
        P(None, "patch", "tm"),
        P(),
        P(None, None, "tm", None),
        P(None, "tm", None),
        P(),
    )
    return jax.shard_map(
        local, mesh=mesh, in_specs=placed, out_specs=P("tm", "patch", None), check_vma=False
    )
```

profile of v0, /device:TPU:0, one launch (start us, length us, event | category | flops | bytes accessed | tf_op | source)
XLA Modules:
  0.0 180.4 jit_solution(3288176917394801471)
XLA Ops:
  6.5 0.0 reduce-scatter.7.cloned.1.call-start
  6.5 0.9 slice_reduce_fusion.1
  7.4 8.8 %all_gather.13 = bf16[4,56,1152]{2,1,0:T(8,128)(2,1)S(1)} all-gather(bf16[1,56,1152]{2,1,0:T(8,128)(2,1)} %param.7), channel_id=1, replica_groups=mesh['tm'=4,'patch'=8] {'tm'}, dimensions={0}, use_global_device_ids=true | all-gather | bytes 645120 | tf_op jit(solution)/shard_map/all_gather | solution.py:52
  16.2 0.1 convert_reduce_fusion.1
  16.3 0.3 fusion.27
  16.6 0.0 copy-start.4
  16.7 2.8 %fusion.9 = f32[3,4,56,288]{3,2,0,1:T(8,128)S(1)} fusion(bf16[2,3,288,1152]{3,2,1,0:T(8,128)(2,1)} %param.11, bf16[4,56,1152]{2,1,0:T(8,128)(2,1)S(1)} %all_gather.13, f32[1152]{0:T(1024)S(1)} %get-tuple-element.6, f32[1152]{0:T(1024)S(1)} %get-tuple-element.7, f32[4,56]{1,0:T(4,128)S(1)} %add_rsqrt_fusion.5, f32[4,56]{1,0:T(4,128)S(1)} %broadcast_multiply_fusion.1), kind=kOutput, calls=%fused_computation.14 | convolution fusion | flops 447455232 | bytes 3291904 | tf_op jit(solution)/shard_map/fpd,ced->cfpe/dot_general | solution.py:32
  19.4 0.0 copy-start.2
  19.4 0.0 copy-start.3
  19.5 0.0 copy-done.4
  19.6 0.1 mul.233
  19.6 0.7 copy-done.2
  20.3 0.7 copy.48
  21.1 0.0 copy-done.3
  21.1 0.1 copy.43
  21.1 0.2 copy.45
  21.4 0.3 squeeze.33
  21.7 0.3 multiply_reduce_fusion.3
  22.0 0.7 add_rsqrt_fusion.3
  22.7 0.3 mul.227
  23.0 0.3 reduce_sum.93
  23.3 0.3 mul.228
  23.6 0.2 mul.229
  23.9 0.9 copy.52
  24.8 35.7 %all_gather.12 = bf16[4,448,288]{2,0,1:T(4,128)(2,1)S(1)} all-gather(bf16[4,56,288]{2,0,1:T(4,128)(2,1)S(1)} %copy.43), channel_id=1, replica_groups=mesh['tm'=4,'patch'=8] {'patch'}, dimensions={1}, use_global_device_ids=true | all-gather | bytes 1161216 | tf_op jit(solution)/shard_map/all_gather | solution.py:57
  60.5 2.3 %copy.44 = bf16[4,448,288]{1,2,0:T(8,128)(2,1)} copy(bf16[4,448,288]{2,0,1:T(4,128)(2,1)S(1)} %all_gather.12) | data formatting | bytes 2064384 | tf_op jit(solution)/shard_map/all_gather | solution.py:57
  62.8 0.0 copy-start.1
  62.8 34.2 %all_gather.14 = bf16[4,448,288]{2,0,1:T(4,128)(2,1)S(1)} all-gather(bf16[4,56,288]{2,0,1:T(4,128)(2,1)} %copy.48), channel_id=1, replica_groups=mesh['tm'=4,'patch'=8] {'patch'}, dimensions={1}, use_global_device_ids=true | all-gather | bytes 1161216 | tf_op jit(solution)/shard_map/all_gather | solution.py:56
  97.0 1.4 copy.51
  98.4 0.0 copy-done.1
  98.4 1.0 multiply_convert_fusion.2
  99.4 3.5 %dynamic_update_slice.6 = bf16[4,448,288]{1,2,0:T(8,128)(2,1)} dynamic-update-slice(bf16[4,448,288]{1,2,0:T(8,128)(2,1)} %copy.44, bf16[4,56,288]{1,2,0:T(8,128)(2,1)S(1)} %copy.45, s32[]{:T(128)} %constant.10.clone.1, s32[]{:T(128)S(6)} %select_n.4, s32[]{:T(128)} %constant.10.clone.1) | dynamic-update-slice | bytes 258052 | tf_op jit(solution)/shard_map/dynamic_update_slice | solution.py:62
  102.9 2.6 %dynamic_update_slice.7 = bf16[4,448,288]{1,2,0:T(8,128)(2,1)S(1)} dynamic-update-slice(bf16[4,448,288]{1,2,0:T(8,128)(2,1)S(1)} %copy.51, bf16[4,56,288]{1,2,0:T(8,128)(2,1)} %copy.52, s32[]{:T(128)} %constant.10.clone.1, s32[]{:T(128)S(6)} %select_n.4, s32[]{:T(128)} %constant.10.clone.1) | dynamic-update-slice | bytes 258052 | tf_op jit(solution)/shard_map/dynamic_update_slice | solution.py:61
  105.5 1.7 fusion.76
  107.2 1.8 fusion.22
  109.1 0.0 copy-start
  109.1 0.1 copy.54
  109.2 0.2 reshape.161
  109.3 2.3 %convolution_convert_fusion.1 = bf16[4,56,1152]{2,1,0:T(8,128)(2,1)} fusion(bf16[4,56,288]{2,1,0:T(8,128)(2,1)S(1)} %reshape.161, bf16[2,288,1152]{2,1,0:T(8,128)(2,1)} %param.12), kind=kOutput, calls=%fused_computation.3 | convolution fusion | flops 148893696 | bytes 1308672 | tf_op jit(solution)/shard_map/fpe,ed->fpd/dot_general | solution.py:72
  111.7 0.0 reduce-scatter.7.cloned.1.call-update
  111.7 0.0 reduce-scatter.9.cloned.1.call-start
  111.8 21.5 %reduce-scatter.7.cloned.1.call-done = bf16[1,56,1152]{2,1,0:T(8,128)(2,1)} async-done(((bf16[4,56,1152]{2,1,0:T(8,128)(2,1)}), bf16[1,56,1152]{2,1,0:T(8,128)(2,1)}) %reduce-scatter.7.cloned.1.call-update) | async-done | bytes 129040
  133.3 0.0 copy-done
  133.3 0.9 add_convert_fusion.1
  134.2 6.9 %all_gather.15 = bf16[4,56,1152]{2,1,0:T(8,128)(2,1)S(1)} all-gather(bf16[1,56,1152]{2,1,0:T(8,128)(2,1)S(1)} %add_convert_fusion.1), channel_id=1, replica_groups=mesh['tm'=4,'patch'=8] {'tm'}, dimensions={0}, use_global_device_ids=true | all-gather | bytes 645120 | tf_op jit(solution)/shard_map/all_gather | solution.py:78
  141.2 0.1 convert_reduce_fusion
  141.3 0.3 fusion.23
  141.6 2.8 %fusion.12 = f32[3,4,56,288]{3,2,0,1:T(8,128)S(1)} fusion(bf16[2,3,288,1152]{3,2,1,0:T(8,128)(2,1)} %param.11, bf16[4,56,1152]{2,1,0:T(8,128)(2,1)S(1)} %all_gather.15, f32[1152]{0:T(1024)S(1)} %get-tuple-element.9, f32[1152]{0:T(1024)S(1)} %get-tuple-element.10, f32[4,56]{1,0:T(4,128)S(1)} %add_rsqrt_fusion.4, f32[4,56]{1,0:T(4,128)S(1)} %broadcast_multiply_fusion), kind=kOutput, calls=%fused_computation.15 | convolution fusion | flops 447455232 | bytes 3291904 | tf_op jit(solution)/shard_map/fpd,ced->cfpe/dot_general | solution.py:32
  144.5 0.2 convert_element_type.113
  144.6 0.3 squeeze.37
  144.9 0.3 multiply_reduce_fusion.2
  145.3 0.3 squeeze.38
  145.6 0.3 multiply_reduce_fusion.1
  145.9 0.5 multiply_convert_fusion
  146.5 0.9 fusion.79
  147.4 0.0 copy-start.5
  147.4 0.5 fusion.21
  147.9 0.1 copy.63
  148.0 0.2 reshape.162
  148.2 0.6 copy-done.5
  148.7 1.2 convolution_convert_fusion
  150.0 0.0 reduce-scatter.9.cloned.1.call-update
  150.0 22.0 %reduce-scatter.9.cloned.1.call-done = bf16[1,56,1152]{2,1,0:T(8,128)(2,1)} async-done(((bf16[4,56,1152]{2,1,0:T(8,128)(2,1)}), bf16[1,56,1152]{2,1,0:T(8,128)(2,1)}) %reduce-scatter.9.cloned.1.call-update) | async-done | bytes 129040
  172.0 1.6 add_convert_fusion
  (14 shorter events, 0.3 us)
Async XLA Ops:
  6.5 126.7 %reduce-scatter.7.cloned.1.call-start = ((), (), s32[]{:S(2)}) async-start(), calls=%async_computation.2 | async-start | bytes 645120
  16.6 2.9 %copy-start.4 = (f32[2,2,72]{2,1,0:T(2,128)S(1)}, f32[2,2,72]{2,1,0:T(2,128)}, u32[]{:S(2)}) copy-start(f32[2,2,72]{2,1,0:T(2,128)} %param.13) | copy-start | bytes 3460
  19.4 0.9 copy-start.2
  19.4 1.6 copy-start.3
  62.8 35.6 %copy-start.1 = (f32[4,56,4]{2,1,0:T(8,128)S(1)}, f32[4,56,4]{2,1,0:T(8,128)}, u32[]{:S(2)}) copy-start(f32[4,56,4]{2,1,0:T(8,128)} %add_rsqrt_fusion.3) | copy-start | bytes 10756
  109.1 24.2 %copy-start = (bf16[1,56,1152]{2,1,0:T(8,128)(2,1)S(1)}, bf16[1,56,1152]{2,1,0:T(8,128)(2,1)}, u32[]{:S(2)}) copy-start(bf16[1,56,1152]{2,1,0:T(8,128)(2,1)} %param.7) | copy-start | bytes 387076
  111.7 60.3 %reduce-scatter.9.cloned.1.call-start = ((), (), s32[]{:S(2)}) async-start(), calls=%async_computation.3 | async-start | bytes 645120
  147.4 1.3 copy-start.5
Sparse Core Ops, SparseCore 0:
  111.8 21.3 reduce-scatter.6
  150.1 21.8 reduce-scatter.8
where the time goes:
time: 181 us; the launch traced here: 180 us
  blocking collectives  85.6 us (47%)
  waiting for transfers between devices  43.5 us (24%)
  local copies, waits for them, and re-layouts  15.6 us (9%)
  matrix products  14 us (8%)
  between operations  13.7 us (8%)
  other arithmetic  7.89 us (4%)
    unnamed x4, waiting for transfers between devices  43.5 us
    all_gather x1, blocking collectives, local(): lax.all_gather(stale_values, 'patch', axis=1, tiled=True)  35.7 us
    all_gather x1, blocking collectives, local(): lax.all_gather(stale_keys, 'patch', axis=1, tiled=True)  34.2 us
    all_gather x1, blocking collectives, local(): lax.all_gather(stream, 'tm', axis=0, tiled=True)  8.79 us
    all_gather x1, blocking collectives, local(): lax.all_gather(middle, 'tm', axis=0, tiled=True)  6.94 us
    dot_general x2, matrix products, projections(): jnp.einsum('fpd,ced->cfpe', hmod, weights, preferred_element_type=jnp.flo...  5.51 us
  transfers between devices with their start and end apart: 2, of which 2 were waited for; matrix products, arithmetic and copies ran while one was open for 0% of the time, Pallas kernels for 0%

commit v1 on v0

v1 whole, which is shorter than its diff:
```python
import functools

import jax
import jax.numpy as jnp
from jax import lax
from jax.experimental import pallas as pl
from jax.experimental.pallas import tpu as pltpu
from jax.sharding import PartitionSpec as P

HEAD_DIM = 72
EPS = 1e-06
MESH = pl.DeviceIdType.MESH
F32 = jnp.float32
BF16 = jnp.bfloat16
NT = (((1,), (1,)), ((), ()))
NN = (((1,), (0,)), ((), ()))


def head_of(index, heads):
    total = jnp.zeros_like(index)
    for head in range(1, heads + 1):
        total = total + jnp.where(index >= head * HEAD_DIM, 1, 0)
    return total


def split_dot(left, right):
    high = left.astype(BF16)
    low = (left - high.astype(F32)).astype(BF16)
    return lax.dot_general(high, right, NN, preferred_element_type=F32) + lax.dot_general(
        low, right, NN, preferred_element_type=F32
    )


def kernel(
    n_tm, n_patch, width, wide,
    stream_ref, old_k_ref, old_v_ref, mod_ref, w_qkv_ref, w_out_ref, gain_ref,
    out_ref,
    wq, wo, own, buf, stage, acc, xg0, xg1, mid, hm, qbd, qkv, attn, part0, part1,
    rp0, rp1, sx0, sx1, rx0, rx1,
    w_sem, kv_send, kv_recv, ag_send_x, ag_send_p, ag_recv, rs_send_p, rs_recv_p, rs_send_x, rs_recv_x,
):
    frames, rows = old_k_ref.shape[0], old_k_ref.shape[1]
    depth = stream_ref.shape[2]
    heads = width // HEAD_DIM
    pad_rows = hm.shape[0] // frames
    held = w_out_ref.shape[1]
    packed = frames * width
    main = rows // 16 * 16
    tail = rows - main
    n_chip = n_tm // 2
    n_line = n_patch // 2
    scale = HEAD_DIM ** (-0.5)

    t = lax.axis_index("tm")
    chip, core = lax.div(t, 2), lax.rem(t, 2)
    partner = chip * 2 + 1 - core
    p = lax.axis_index("patch")
    a, b = lax.div(p, 2), lax.rem(p, 2)
    beside = a * 2 + 1 - b

    def other_chip(j):
        return lax.rem(chip + j, n_chip)

    loads = []
    for block in range(2):
        for c in range(3):
            loads.append(pltpu.make_async_copy(
                w_qkv_ref.at[block, c], wq.at[block, c, pl.ds(0, held)], w_sem.at[block * 4 + c]))
        loads.append(pltpu.make_async_copy(
            w_out_ref.at[block], wo.at[block, pl.ds(0, held)], w_sem.at[block * 4 + 3]))
    for load in loads:
        load.start()

    barrier = pltpu.get_barrier_semaphore()

    def greet(**where):
        pl.semaphore_signal(barrier, inc=1, device_id=where, device_id_type=MESH)

    greet(tm=partner)
    greet(patch=beside)
    for j in range(1, n_chip):
        greet(tm=other_chip(j) * 2 + core)

    @pl.when(a > 0)
    def _():
        greet(patch=p - 2)

    @pl.when(a < n_line - 1)
    def _():
        greet(patch=p + 2)

    met = 1 + n_chip + jnp.where(a > 0, 1, 0) + jnp.where(a < n_line - 1, 1, 0)
    pl.semaphore_wait(barrier, met)

    def remote(src, dst, send, recv, where):
        return pltpu.make_async_remote_copy(
            src_ref=src, dst_ref=dst, send_sem=send, recv_sem=recv, device_id=where, device_id_type=MESH)

    def gather_start(block, src, xg):
        sends = []
        for j in range(1, n_chip):
            sends.append(remote(src, xg.at[t], ag_send_x.at[block, j], ag_recv.at[block, t],
                                {"tm": other_chip(j) * 2 + core}))
        sends.append(remote(src, xg.at[t], ag_send_p.at[block, 0], ag_recv.at[block, t], {"tm": partner}))
        for send in sends:
            send.start()
        return sends

    def gather_arrived(block, xg, frame):
        remote(xg.at[frame], xg.at[frame], ag_send_p.at[block, 0], ag_recv.at[block, frame],
               {"tm": partner}).wait_recv()

    def gather_forward(block, xg):
        sends = []
        for j in range(1, n_chip):
            frame = other_chip(j) * 2 + core
            gather_arrived(block, xg, frame)
            send = remote(xg.at[frame], xg.at[frame], ag_send_p.at[block, j], ag_recv.at[block, frame],
                          {"tm": partner})
            send.start()
            sends.append(send)
        return sends

    def gather_finish(block, xg):
        for j in range(n_chip):
            gather_arrived(block, xg, other_chip(j) * 2 + 1 - core)

    pending = gather_start(0, stream_ref.at[0], xg0)
    xg0[t] = stream_ref[0]

    def window(frame):
        low = min(frame * width // 128 * 128, packed - wide)
        return low, frame * width - low

    def pack(slot):
        keys, values = acc[0], acc[1]
        slot[...] = jnp.concatenate(
            [keys[:main], values[:main], keys[main:], values[main:]], axis=0).astype(BF16)

    def place(which, frame, value):
        low, offset = window(frame)
        if offset:
            value = pltpu.roll(value, offset, 1)
        acc[which, :, low:low + wide] += value

    acc[...] = jnp.zeros_like(acc)
    stage[...] = jnp.zeros_like(stage)
    for frame in range(frames):
        for which, ref in enumerate((old_k_ref, old_v_ref)):
            stage[which, :, 0:width] = ref[frame].astype(F32)
            place(which, frame, stage[which])
    pack(own)

    def kv_copy(src, piece, kind, step, where):
        return remote(src, buf.at[piece], kv_send.at[kind, step], kv_recv.at[piece], {"patch": where})

    def relay(step, go):
        for kind, sign in ((0, 1), (1, -1)):
            origin = a - sign * step
            onward = a + sign
            piece = jnp.clip(origin, 0, n_line - 1) * 2 + b
            src = own if step == 0 else buf.at[piece]
            here = (origin >= 0) & (origin < n_line)

            @pl.when(here)
            def _():
                if step and go:
                    kv_copy(src, piece, kind, step, beside).wait_recv()
                if step:
                    across = kv_copy(src, piece, 2 + kind, step, beside)
                    across.start() if go else across.wait_send()

            @pl.when(here & (onward >= 0) & (onward < n_line))
            def _():
                along = kv_copy(src, piece, kind, step, jnp.clip(onward, 0, n_line - 1) * 2 + b)
                along.start() if go else along.wait_send()
        if step == 0:
            across = kv_copy(own, p, 2, 0, beside)
            across.start() if go else across.wait_send()

    relay(0, True)

    features = lax.broadcasted_iota(jnp.int32, (wide, wide), 0)
    columns = lax.broadcasted_iota(jnp.int32, (wide, wide), 1)
    same_head = (head_of(features, heads) == head_of(columns, heads)) & (features < width) & (columns < width)
    group = jnp.where(same_head, 1.0, 0.0).astype(BF16)
    lane = lax.broadcasted_iota(jnp.int32, (1, wide), 1)
    lane_head = head_of(lane, heads)
    down = lax.broadcasted_iota(jnp.int32, (HEAD_DIM, wide), 0)
    over = lax.broadcasted_iota(jnp.int32, (HEAD_DIM, wide), 1)
    over_head = head_of(over, heads)
    spread = jnp.where((over - HEAD_DIM * over_head == down) & (over_head < heads), 1.0, 0.0).astype(BF16)

    def gain_row(block, which):
        gain = gain_ref[block, which:which + 1, :]
        first = gain.astype(BF16)
        rest = gain - first.astype(F32)
        return lax.dot_general(first, spread, NN, preferred_element_type=F32) + split_dot(rest, spread)

    if wide > held:
        wq[:, :, held:, :] = jnp.zeros((2, 3, wide - held, depth), BF16)
        wo[:, held:, :] = jnp.zeros((2, wide - held, depth), BF16)

    def modulated(block, xg):
        shift, gain = mod_ref[block, 0:1], 1.0 + mod_ref[block, 1:2]
        for frame in range(frames):
            values = xg[frame].astype(F32)
            center = jnp.mean(values, axis=-1, keepdims=True)
            values = values - center
            spread_ = jnp.mean(values * values, axis=-1, keepdims=True)
            hmod = values * lax.rsqrt(spread_ + EPS) * gain + shift
            hmod = jnp.concatenate([hmod, jnp.zeros((pad_rows - rows, depth), F32)], axis=0)
            hm[frame * pad_rows:(frame + 1) * pad_rows, :] = hmod.astype(BF16)

    def projections(block):
        for c in range(3):
            loads[block * 4 + c].wait()
            raw = lax.dot_general(hm[...], wq[block, c], NT, preferred_element_type=F32)
            if c < 2:
                square = split_dot(raw * raw, group) * (1.0 / HEAD_DIM)
                raw = raw * lax.rsqrt(square + EPS) * gain_row(block, c)
            qkv[c] = raw

    def heads_out(block, part):
        loads[block * 4 + 3].wait()
        product = lax.dot_general(attn[...], wo[block], NN, preferred_element_type=F32)
        for frame in range(frames):
            part[frame] = product[frame * pad_rows:frame * pad_rows + rows].astype(BF16)

    def attn_store(frame, value):
        value = jnp.concatenate([value, jnp.zeros((pad_rows - rows, wide), F32)], axis=0)
        attn[frame * pad_rows:(frame + 1) * pad_rows, :] = value.astype(BF16)

    def reduced(block, part, rp, sx, rx):
        sends = []
        for j in list(range(1, n_chip)) + [0]:
            to = other_chip(j)
            send = remote(part.at[to * 2 + 1 - core], rp.at[to], rs_send_p.at[block, j], rs_recv_p.at[block, to],
                          {"tm": partner})
            send.start()
            sends.append(send)

        def arrived(to):
            remote(rp.at[to], rp.at[to], rs_send_p.at[block, 0], rs_recv_p.at[block, to],
                   {"tm": partner}).wait_recv()

        for j in range(1, n_chip):
            to = other_chip(j)
            arrived(to)
            sx[j - 1] = (part[to * 2 + core].astype(F32) + rp[to].astype(F32)).astype(BF16)
            send = remote(sx.at[j - 1], rx.at[j - 1], rs_send_x.at[block, j - 1], rs_recv_x.at[block, j - 1],
                          {"tm": to * 2 + core})
            send.start()
            sends.append(send)
        arrived(chip)
        total = part[t].astype(F32) + rp[chip].astype(F32)
        for j in range(1, n_chip):
            remote(sx.at[j - 1], rx.at[j - 1], rs_send_x.at[block, j - 1], rs_recv_x.at[block, j - 1],
                   {"tm": t}).wait_recv()
            total = total + rx[j - 1].astype(F32)
        return total, sends

    pending += gather_forward(0, xg0)
    gather_finish(0, xg0)
    modulated(0, xg0)
    if n_line > 1:
        relay(1, True)
    projections(0)
    acc[...] = jnp.zeros_like(acc)
    for frame in range(frames):
        start = frame * pad_rows
        for which in range(2):
            place(which, frame, qkv[1 + which, start:start + rows])
        _, offset = window(frame)
        query = qkv[0, start:start + rows]
        stacked = jnp.concatenate([jnp.where(lane_head == head, query, 0.0) for head in range(heads)], axis=0)
        if offset:
            stacked = pltpu.roll(stacked, offset, 1)
        qbd[frame] = stacked.astype(BF16)
    pack(buf.at[p])
    for step in range(2, n_line):
        relay(step, True)
    for line in range(n_line):
        piece = line * 2 + 1 - b
        kv_copy(own, piece, 2, 0, beside).wait_recv()

    spot = lax.broadcasted_iota(jnp.int32, (1, n_patch * 2 * tail), 1)
    real = (lax.rem(spot, 2 * tail) < tail)
    for frame in range(frames):
        low, offset = window(frame)
        keys = buf[:, 0:main, low:low + wide].reshape(n_patch * main, wide)
        values = buf[:, main:2 * main, low:low + wide].reshape(n_patch * main, wide)
        rest = buf[:, 2 * main:, low:low + wide].reshape(n_patch * 2 * tail, wide)
        query = qbd[frame]
        first = lax.dot_general(query, keys, NT, preferred_element_type=F32)
        second = lax.dot_general(query, rest, NT, preferred_element_type=F32)
        second = jnp.where(real, second, -1e30)
        top = jnp.maximum(jnp.max(first, axis=-1, keepdims=True), jnp.max(second, axis=-1, keepdims=True))
        first = jnp.exp((first - top) * scale)
        second = jnp.exp((second - top) * scale)
        norm = jnp.sum(first, axis=-1, keepdims=True) + jnp.sum(second, axis=-1, keepdims=True)
        second = pltpu.roll(second, tail, 1)
        mixed = lax.dot_general(first.astype(BF16), values, NN, preferred_element_type=F32)
        mixed = mixed + lax.dot_general(second.astype(BF16), rest, NN, preferred_element_type=F32)
        mixed = mixed / norm
        total = jnp.zeros((rows, wide), F32)
        for head in range(heads):
            start = offset + head * HEAD_DIM
            inside = (lane >= start) & (lane < start + HEAD_DIM)
            total = total + jnp.where(inside, mixed[head * rows:(head + 1) * rows], 0.0)
        if offset:
            total = pltpu.roll(total, wide - offset, 1)
        attn_store(frame, total)
    heads_out(0, part0)
    summed, sends = reduced(0, part0, rp0, sx0, rx0)
    pending += sends
    middle = (stream_ref[0].astype(F32) + mod_ref[0, 2:3] * summed).astype(BF16)
    mid[...] = middle
    pending += gather_start(1, mid, xg1)
    xg1[t] = middle

    pending += gather_forward(1, xg1)
    gather_finish(1, xg1)
    modulated(1, xg1)
    projections(1)
    for frame in range(frames):
        query = qkv[0, frame * pad_rows:frame * pad_rows + rows].astype(BF16).astype(F32)
        scores = []
        products = jnp.concatenate([
            query * qkv[1, g * pad_rows:g * pad_rows + rows].astype(BF16).astype(F32) for g in range(frames)], axis=0)
        products = split_dot(products, group) * scale
        scores = [products[g * rows:(g + 1) * rows] for g in range(frames)]
        top = functools.reduce(jnp.maximum, scores)
        scores = [jnp.exp(score - top) for score in scores]
        norm = 1.0 / functools.reduce(jnp.add, scores)
        total = jnp.zeros((rows, wide), F32)
        for g in range(frames):
            weight = (scores[g] * norm).astype(BF16).astype(F32)
            total = total + weight * qkv[2, g * pad_rows:g * pad_rows + rows].astype(BF16).astype(F32)
        attn_store(frame, total)
    heads_out(1, part1)
    summed, sends = reduced(1, part1, rp1, sx1, rx1)
    pending += sends
    out_ref[0] = (mid[...].astype(F32) + mod_ref[1, 2:3] * summed).astype(BF16)

    for send in pending:
        send.wait_send()
    for step in range(n_line):
        relay(step, False)


def local(n_tm, n_patch, stream, stale_keys, stale_values, modulation, w_qkv, w_out, qk_gain):
    frames, rows, width = stale_keys.shape
    depth = stream.shape[2]
    extra = -width % 16
    if extra:
        w_qkv = jnp.pad(w_qkv, ((0, 0), (0, 0), (0, extra), (0, 0)))
        w_out = jnp.pad(w_out, ((0, 0), (0, extra), (0, 0)))
    wide = max((frame * width % 128 + width + 127) // 128 * 128 for frame in range(frames))
    pad_rows = (rows + 15) // 16 * 16
    heads = width // HEAD_DIM
    n_chip, n_line = n_tm // 2, n_patch // 2
    vmem = pl.BlockSpec(memory_space=pltpu.VMEM)
    hbm = pl.BlockSpec(memory_space=pl.ANY)
    far = max(n_chip - 1, 1)
    return pl.pallas_call(
        functools.partial(kernel, n_tm, n_patch, width, wide),
        out_shape=jax.ShapeDtypeStruct(stream.shape, BF16),
        in_specs=[vmem, vmem, vmem, vmem, hbm, hbm, vmem],
        out_specs=vmem,
        scratch_shapes=[
            pltpu.VMEM((2, 3, wide, depth), BF16),
            pltpu.VMEM((2, wide, depth), BF16),
            pltpu.VMEM((2 * rows, frames * width), BF16),
            pltpu.VMEM((n_patch, 2 * rows, frames * width), BF16),
            pltpu.VMEM((2, rows, wide), F32),
            pltpu.VMEM((2, rows, frames * width), F32),
            pltpu.VMEM((frames, rows, depth), BF16),
            pltpu.VMEM((frames, rows, depth), BF16),
            pltpu.VMEM((rows, depth), BF16),
            pltpu.VMEM((frames * pad_rows, depth), BF16),
            pltpu.VMEM((frames, heads * rows, wide), BF16),
            pltpu.VMEM((3, frames * pad_rows, wide), F32),
            pltpu.VMEM((frames * pad_rows, wide), BF16),
            pltpu.VMEM((frames, rows, depth), BF16),
            pltpu.VMEM((frames, rows, depth), BF16),
            pltpu.VMEM((n_chip, rows, depth), BF16),
            pltpu.VMEM((n_chip, rows, depth), BF16),
            pltpu.VMEM((far, rows, depth), BF16),
            pltpu.VMEM((far, rows, depth), BF16),
            pltpu.VMEM((far, rows, depth), BF16),
            pltpu.VMEM((far, rows, depth), BF16),
            pltpu.SemaphoreType.DMA((8,)),
            pltpu.SemaphoreType.DMA((4, n_line)),
            pltpu.SemaphoreType.DMA((n_patch,)),
            pltpu.SemaphoreType.DMA((2, n_chip)),
            pltpu.SemaphoreType.DMA((2, n_chip)),
            pltpu.SemaphoreType.DMA((2, n_tm)),
            pltpu.SemaphoreType.DMA((2, n_chip)),
            pltpu.SemaphoreType.DMA((2, n_chip)),
            pltpu.SemaphoreType.DMA((2, far)),
            pltpu.SemaphoreType.DMA((2, far)),
        ],
        compiler_params=pltpu.CompilerParams(
            collective_id=0, has_side_effects=True, vmem_limit_bytes=48 * 1024 * 1024),
        cost_estimate=pl.CostEstimate(flops=4_000_000_000, bytes_accessed=8_000_000, transcendentals=1_000_000),
    )(stream, stale_keys, stale_values, modulation, w_qkv, w_out, qk_gain)


def solution(mesh):
    placed = (
        P("tm", "patch", None),
        P(None, "patch", "tm"),
        P(None, "patch", "tm"),
        P(),
        P(None, None, "tm", None),
        P(None, "tm", None),
        P(),
    )
    return jax.shard_map(
        functools.partial(local, mesh.shape["tm"], mesh.shape["patch"]),
        mesh=mesh, in_specs=placed, out_specs=P("tm", "patch", None), check_vma=False,
    )
```

time: 181 us -> 65.8 us (0.36)
  blocking collectives: 85.6 us -> 0 us
  Pallas kernels: 0 us -> 57.2 us
  waiting for transfers between devices: 43.5 us -> 0 us
  matrix products: 14 us -> 0 us
  between operations: 13.7 us -> 0.03 us
  other arithmetic: 7.89 us -> 0 us
  local copies, waits for them, and re-layouts: 15.6 us -> 8.27 us
    all_gather x4 -> x0, blocking collectives: 85.6 us -> none  [the longest x1 35.7 us: local(): lax.all_gather(stale_values, 'patch', axis=1, tiled=True)]
    pallas_call x0 -> x1, Pallas kernels: none -> 57.2 us  [local(): pl.pallas_call(functools.partial(kernel, n_tm, n_patch, width, wide), out...]
    unnamed x4 -> x0, waiting for transfers between devices: 43.5 us -> none
    dot_general x6 -> x0, matrix products: 11.4 us -> none  [the longest x2 5.51 us: projections(): jnp.einsum('fpd,ced->cfpe', hmod, weights, preferred_element_type=jnp.flo...]
    unnamed x14, local copies, waits for them, and re-layouts: 2.08 us -> 8.27 us
    dynamic_update_slice x2 -> x0, local copies, waits for them, and re-layouts: 6.11 us -> none  [the longest x1 3.48 us: local(): values = lax.dynamic_update_slice_in_dim(old_values, packed[2], offset, 1)]
    convert_element_type x5 -> x0, other arithmetic: 4.1 us -> none  [the longest x1 1.59 us: local(): (middle.astype(jnp.float32) + modulation[1, 2] * summed_out).astype(jnp.b...]
    all_gather x2 -> x0, local copies, waits for them, and re-layouts: 3.72 us -> none  [the longest x1 2.28 us: local(): lax.all_gather(stale_values, 'patch', axis=1, tiled=True)]
  transfers between devices with their start and end apart: 2 -> 0, of which waited for: 2 -> 0; matrix products, arithmetic and copies ran while one was open for 0% -> 0% of each run, Pallas kernels for 0% -> 0%
where the time goes in v1:
time: 65.8 us; the launch traced here: 65.5 us
  Pallas kernels  57.2 us (87%)
  local copies, waits for them, and re-layouts  8.27 us (13%)
    pallas_call x1, Pallas kernels, local(): pl.pallas_call(functools.partial(kernel, n_tm, n_patch, width, wide), out...  57.2 us
    unnamed x14, local copies, waits for them, and re-layouts  8.27 us

profile of v1, /device:TPU:0, one launch (start us, length us, event | category | flops | bytes accessed | tf_op | source)
XLA Modules:
  0.0 65.5 jit_solution(4990282193678104438)
XLA Ops:
  0.0 0.8 %copy.8.mod_ref = f32[2,3,1152]{2,1,0:T(4,128)S(1)} copy(f32[2,3,1152]{2,0,1:T(2,128)} %param.10) | data formatting | bytes 55296 | tf_op args[3]
  0.8 0.0 copy-start
  0.8 2.1 %copy-done = bf16[2,3,288,1152]{3,2,1,0:T(8,128)(2,1)S(1)} copy-done((bf16[2,3,288,1152]{3,2,1,0:T(8,128)(2,1)S(1)}, bf16[2,3,288,1152]{3,2,1,0:T(8,128)(2,1)}, u32[]{:S(2)}) %copy-start) | copy-done | bytes 3981336
  2.9 0.0 copy-start.1
  2.9 1.3 %copy-done.1 = bf16[2,288,1152]{2,1,0:T(8,128)(2,1)S(1)} copy-done((bf16[2,288,1152]{2,1,0:T(8,128)(2,1)S(1)}, bf16[2,288,1152]{2,1,0:T(8,128)(2,1)}, u32[]{:S(2)}) %copy-start.1) | copy-done | bytes 1327128
  4.2 0.0 copy-start.2
  4.2 0.9 %copy-done.2 = bf16[4,56,288]{2,1,0:T(8,128)(2,1)S(1)} copy-done((bf16[4,56,288]{2,1,0:T(8,128)(2,1)S(1)}, bf16[4,56,288]{2,1,0:T(8,128)(2,1)}, u32[]{:S(2)}) %copy-start.2) | copy-done | bytes 129048
  5.1 0.0 copy-start.3
  5.1 0.9 %copy-done.3 = bf16[4,56,288]{2,1,0:T(8,128)(2,1)S(1)} copy-done((bf16[4,56,288]{2,1,0:T(8,128)(2,1)S(1)}, bf16[4,56,288]{2,1,0:T(8,128)(2,1)}, u32[]{:S(2)}) %copy-start.3) | copy-done | bytes 129048
  6.0 0.0 copy-start.4
  6.1 0.9 %copy-done.4 = bf16[1,56,1152]{2,1,0:T(8,128)(2,1)S(1)} copy-done((bf16[1,56,1152]{2,1,0:T(8,128)(2,1)S(1)}, bf16[1,56,1152]{2,1,0:T(8,128)(2,1)}, u32[]{:S(2)}) %copy-start.4) | copy-done | bytes 129048
  7.0 0.0 copy-start.5
  7.0 0.7 %copy-done.5 = f32[2,2,72]{2,1,0:T(2,128)S(1)} copy-done((f32[2,2,72]{2,1,0:T(2,128)S(1)}, f32[2,2,72]{2,1,0:T(2,128)}, u32[]{:S(2)}) %copy-start.5) | copy-done | bytes 1176
  7.6 57.2 %shard_map.73 = bf16[1,56,1152]{2,1,0:T(8,128)(2,1)S(1)} custom-call(bf16[1,56,1152]{2,1,0:T(8,128)(2,1)S(1)} %copy-done.4, bf16[4,56,288]{2,1,0:T(8,128)(2,1)S(1)} %copy-done.2, bf16[4,56,288]{2,1,0:T(8,128)(2,1)S(1)} %copy-done.3, f32[2,3,1152]{2,1,0:T(4,128)S(1)} %copy.8.mod_ref, bf16[2,3,288,1152]{3,2,1,0:T(8,128)(2,1)S(1)} %copy-done, ...), custom_call_target="tpu_custom_call" | custom-call | flops 4000000000 | bytes 8000000 | tf_op jit(solution)/shard_map/pallas_call | solution.py:366
  64.8 0.7 copy.10
Async XLA Ops:
  0.8 2.1 %copy-start = (bf16[2,3,288,1152]{3,2,1,0:T(8,128)(2,1)S(1)}, bf16[2,3,288,1152]{3,2,1,0:T(8,128)(2,1)}, u32[]{:S(2)}) copy-start(bf16[2,3,288,1152]{3,2,1,0:T(8,128)(2,1)} %w_qkv_ref.1) | copy-start | bytes 11943940
  2.9 1.3 %copy-start.1 = (bf16[2,288,1152]{2,1,0:T(8,128)(2,1)S(1)}, bf16[2,288,1152]{2,1,0:T(8,128)(2,1)}, u32[]{:S(2)}) copy-start(bf16[2,288,1152]{2,1,0:T(8,128)(2,1)} %w_out_ref.1) | copy-start | bytes 3981316
  4.2 0.9 %copy-start.2 = (bf16[4,56,288]{2,1,0:T(8,128)(2,1)S(1)}, bf16[4,56,288]{2,1,0:T(8,128)(2,1)}, u32[]{:S(2)}) copy-start(bf16[4,56,288]{2,1,0:T(8,128)(2,1)} %old_k_ref.1) | copy-start | bytes 387076
  5.1 0.9 %copy-start.3 = (bf16[4,56,288]{2,1,0:T(8,128)(2,1)S(1)}, bf16[4,56,288]{2,1,0:T(8,128)(2,1)}, u32[]{:S(2)}) copy-start(bf16[4,56,288]{2,1,0:T(8,128)(2,1)} %old_v_ref.1) | copy-start | bytes 387076
  6.0 0.9 %copy-start.4 = (bf16[1,56,1152]{2,1,0:T(8,128)(2,1)S(1)}, bf16[1,56,1152]{2,1,0:T(8,128)(2,1)}, u32[]{:S(2)}) copy-start(bf16[1,56,1152]{2,1,0:T(8,128)(2,1)} %stream_ref.1) | copy-start | bytes 387076
  7.0 0.7 %copy-start.5 = (f32[2,2,72]{2,1,0:T(2,128)S(1)}, f32[2,2,72]{2,1,0:T(2,128)}, u32[]{:S(2)}) copy-start(f32[2,2,72]{2,1,0:T(2,128)} %gain_ref.1) | copy-start | bytes 3460

commit v2 on v1

v2 whole, which is shorter than its diff:
```python
import functools

import jax
import jax.numpy as jnp
from jax import lax
from jax.experimental import pallas as pl
from jax.experimental.pallas import tpu as pltpu
from jax.sharding import PartitionSpec as P

HEAD_DIM = 72
EPS = 1e-06
MESH = pl.DeviceIdType.MESH
F32 = jnp.float32
BF16 = jnp.bfloat16
NT = (((1,), (1,)), ((), ()))
NN = (((1,), (0,)), ((), ()))


def head_of(index, heads):
    total = jnp.zeros_like(index)
    for head in range(1, heads + 1):
        total = total + jnp.where(index >= head * HEAD_DIM, 1, 0)
    return total


def split_dot(left, right):
    high = left.astype(BF16)
    low = (left - high.astype(F32)).astype(BF16)
    return lax.dot_general(high, right, NN, preferred_element_type=F32) + lax.dot_general(
        low, right, NN, preferred_element_type=F32
    )


def kernel(
    n_tm, n_patch, width, wide, parts,
    stream_ref, old_k_ref, old_v_ref, mod_ref, w_qkv_ref, w_out_ref, gain_ref,
    out_ref,
    wq, wo, old, mod, gains, own, buf, stage, acc, xg0, *rest_refs,
):
    n_part = len(parts)
    rest_refs = list(rest_refs)

    def take():
        return [rest_refs.pop(0) for _ in range(n_part)]

    xg1, mid, qbd = take(), take(), take()
    partial = [take(), take()]
    rp, sx, rx = [take(), take()], [take(), take()], [take(), take()]
    (w_sem, in_sem, kv_send, kv_recv, ag_send_x, ag_send_p, ag_recv,
     rs_send_p, rs_recv_p, rs_send_x, rs_recv_x) = rest_refs
    frames, rows = old_k_ref.shape[0], old_k_ref.shape[1]
    depth = stream_ref.shape[2]
    heads = width // HEAD_DIM
    held = w_out_ref.shape[1]
    packed = frames * width
    main = rows // 16 * 16
    tail = rows - main
    n_chip = n_tm // 2
    n_line = n_patch // 2
    scale = HEAD_DIM ** (-0.5)

    t = lax.axis_index("tm")
    chip, core = lax.div(t, 2), lax.rem(t, 2)
    partner = chip * 2 + 1 - core
    p = lax.axis_index("patch")
    a, b = lax.div(p, 2), lax.rem(p, 2)
    beside = a * 2 + 1 - b

    def other_chip(j):
        return lax.rem(chip + j, n_chip)

    inputs = [
        pltpu.make_async_copy(old_k_ref, old.at[0], in_sem.at[0]),
        pltpu.make_async_copy(old_v_ref, old.at[1], in_sem.at[1]),
        pltpu.make_async_copy(stream_ref.at[0], xg0.at[t], in_sem.at[2]),
        pltpu.make_async_copy(mod_ref, mod, in_sem.at[3]),
        pltpu.make_async_copy(gain_ref, gains, in_sem.at[4]),
    ]
    loads = []
    for block in range(2):
        for c in range(3):
            loads.append(pltpu.make_async_copy(
                w_qkv_ref.at[block, c], wq.at[block, c, pl.ds(0, held)], w_sem.at[block * 4 + c]))
        loads.append(pltpu.make_async_copy(
            w_out_ref.at[block], wo.at[block, pl.ds(0, held)], w_sem.at[block * 4 + 3]))
    for load in inputs + loads:
        load.start()

    barrier = pltpu.get_barrier_semaphore()

    def greet(**where):
        pl.semaphore_signal(barrier, inc=1, device_id=where, device_id_type=MESH)

    greet(tm=partner)
    greet(patch=beside)
    for j in range(1, n_chip):
        greet(tm=other_chip(j) * 2 + core)

    @pl.when(a > 0)
    def _():
        greet(patch=p - 2)

    @pl.when(a < n_line - 1)
    def _():
        greet(patch=p + 2)

    def window(frame):
        low = min(frame * width // 128 * 128, packed - wide)
        return low, frame * width - low

    def pack(slot):
        keys, values = acc[0], acc[1]
        slot[...] = jnp.concatenate(
            [keys[:main], values[:main], keys[main:], values[main:]], axis=0).astype(BF16)

    def place(which, frame, value):
        low, offset = window(frame)
        if offset:
            value = pltpu.roll(value, offset, 1)
        acc[which, :, low:low + wide] += value

    acc[...] = jnp.zeros_like(acc)
    stage[...] = jnp.zeros_like(stage)
    for which in range(2):
        inputs[which].wait()
        for frame in range(frames):
            stage[which, :, 0:width] = old[which, frame].astype(F32)
            place(which, frame, stage[which])
    pack(own)

    met = 1 + n_chip + jnp.where(a > 0, 1, 0) + jnp.where(a < n_line - 1, 1, 0)
    pl.semaphore_wait(barrier, met)

    def remote(src, dst, send, recv, where):
        return pltpu.make_async_remote_copy(
            src_ref=src, dst_ref=dst, send_sem=send, recv_sem=recv, device_id=where, device_id_type=MESH)

    pending = []

    def started(copy):
        copy.start()
        pending.append(copy)

    def kv_copy(src, piece, kind, step, where):
        return remote(src, buf.at[piece], kv_send.at[kind, step], kv_recv.at[piece], {"patch": where})

    def relay(step, go):
        for kind, sign in ((0, 1), (1, -1)):
            origin = a - sign * step
            onward = a + sign
            piece = jnp.clip(origin, 0, n_line - 1) * 2 + b
            src = own if step == 0 else buf.at[piece]
            here = (origin >= 0) & (origin < n_line)

            @pl.when(here)
            def _():
                if step and go:
                    kv_copy(src, piece, kind, step, beside).wait_recv()
                if step:
                    across = kv_copy(src, piece, 2 + kind, step, beside)
                    across.start() if go else across.wait_send()

            @pl.when(here & (onward >= 0) & (onward < n_line))
            def _():
                along = kv_copy(src, piece, kind, step, jnp.clip(onward, 0, n_line - 1) * 2 + b)
                along.start() if go else along.wait_send()
        if step == 0:
            across = kv_copy(own, p, 2, 0, beside)
            across.start() if go else across.wait_send()

    relay(0, True)

    def gather_start(phase, src, xg):
        for j in range(1, n_chip):
            started(remote(src, xg.at[t], ag_send_x.at[phase, j], ag_recv.at[phase, t],
                           {"tm": other_chip(j) * 2 + core}))
        started(remote(src, xg.at[t], ag_send_p.at[phase, 0], ag_recv.at[phase, t], {"tm": partner}))

    def gather_arrived(phase, xg, frame):
        remote(xg.at[frame], xg.at[frame], ag_send_p.at[phase, 0], ag_recv.at[phase, frame],
               {"tm": partner}).wait_recv()

    def gather_forward(phase, xg):
        for j in range(1, n_chip):
            frame = other_chip(j) * 2 + core
            gather_arrived(phase, xg, frame)
            started(remote(xg.at[frame], xg.at[frame], ag_send_p.at[phase, j], ag_recv.at[phase, frame],
                           {"tm": partner}))

    def gather_finish(phase, xg):
        for j in range(n_chip):
            gather_arrived(phase, xg, other_chip(j) * 2 + 1 - core)

    inputs[2].wait()
    gather_start(0, xg0.at[t], xg0)

    features = lax.broadcasted_iota(jnp.int32, (wide, wide), 0)
    columns = lax.broadcasted_iota(jnp.int32, (wide, wide), 1)
    same_head = (head_of(features, heads) == head_of(columns, heads)) & (features < width) & (columns < width)
    group = jnp.where(same_head, 1.0, 0.0).astype(BF16)
    lane = lax.broadcasted_iota(jnp.int32, (1, wide), 1)
    lane_head = head_of(lane, heads)
    down = lax.broadcasted_iota(jnp.int32, (HEAD_DIM, wide), 0)
    over = lax.broadcasted_iota(jnp.int32, (HEAD_DIM, wide), 1)
    over_head = head_of(over, heads)
    spread = jnp.where((over - HEAD_DIM * over_head == down) & (over_head < heads), 1.0, 0.0).astype(BF16)

    def gain_row(block, which):
        gain = gains[block, which:which + 1, :]
        first = gain.astype(BF16)
        rest = gain - first.astype(F32)
        return lax.dot_general(first, spread, NN, preferred_element_type=F32) + split_dot(rest, spread)

    if wide > held:
        wq[:, :, held:, :] = jnp.zeros((2, 3, wide - held, depth), BF16)
        wo[:, held:, :] = jnp.zeros((2, wide - held, depth), BF16)
    inputs[3].wait()
    inputs[4].wait()
    gain_rows = [[gain_row(block, c) for c in range(2)] for block in range(2)]

    def modulated(block, xg):
        shift, gain = mod[0, block:block + 1], 1.0 + mod[1, block:block + 1]
        out = []
        for frame in range(frames):
            values = xg[frame].astype(F32)
            center = jnp.mean(values, axis=-1, keepdims=True)
            values = values - center
            spread_ = jnp.mean(values * values, axis=-1, keepdims=True)
            out.append(values * lax.rsqrt(spread_ + EPS) * gain + shift)
        return jnp.concatenate(out, axis=0).astype(BF16)

    def projections(block, hmod):
        raw = lax.dot_general(
            hmod, wq[block].reshape(3 * wide, depth), NT, preferred_element_type=F32)
        out = []
        for c in range(2):
            piece = raw[:, c * wide:(c + 1) * wide]
            square = split_dot(piece * piece, group) * (1.0 / HEAD_DIM)
            out.append(piece * lax.rsqrt(square + EPS) * gain_rows[block][c])
        return out + [raw[:, 2 * wide:]]

    def heads_out(block, half, attn):
        count = parts[half][1]
        product = lax.dot_general(
            jnp.concatenate(attn, axis=0).astype(BF16), wo[block], NN, preferred_element_type=F32)
        for frame in range(frames):
            partial[block][half][frame] = product[frame * count:(frame + 1) * count].astype(BF16)

    def sum_start(block, half):
        phase = block * n_part + half
        part, inbox = partial[block][half], rp[block][half]
        for j in list(range(1, n_chip)) + [0]:
            to = other_chip(j)
            started(remote(part.at[to * 2 + 1 - core], inbox.at[to], rs_send_p.at[phase, j], rs_recv_p.at[phase, to],
                           {"tm": partner}))

    def sum_arrived(phase, inbox, to):
        remote(inbox.at[to], inbox.at[to], rs_send_p.at[phase, 0], rs_recv_p.at[phase, to],
               {"tm": partner}).wait_recv()

    def sum_across(block, half):
        phase = block * n_part + half
        part, inbox, outbox = partial[block][half], rp[block][half], sx[block][half]
        for j in range(1, n_chip):
            to = other_chip(j)
            sum_arrived(phase, inbox, to)
            outbox[j - 1] = (part[to * 2 + core].astype(F32) + inbox[to].astype(F32)).astype(BF16)
            started(remote(outbox.at[j - 1], rx[block][half].at[j - 1], rs_send_x.at[phase, j - 1],
                           rs_recv_x.at[phase, j - 1], {"tm": to * 2 + core}))

    def sum_finish(block, half):
        phase = block * n_part + half
        sum_arrived(phase, rp[block][half], chip)
        total = partial[block][half][t].astype(F32) + rp[block][half][chip].astype(F32)
        for j in range(1, n_chip):
            remote(sx[block][half].at[j - 1], rx[block][half].at[j - 1], rs_send_x.at[phase, j - 1],
                   rs_recv_x.at[phase, j - 1], {"tm": partner}).wait_recv()
            total = total + rx[block][half][j - 1].astype(F32)
        return total

    gather_forward(0, xg0)
    gather_finish(0, xg0)
    hmod = modulated(0, xg0)
    if n_line > 1:
        relay(1, True)
    for load in loads[:3]:
        load.wait()
    query, keys, values = projections(0, hmod)
    acc[...] = jnp.zeros_like(acc)
    for frame in range(frames):
        place(0, frame, keys[frame * rows:(frame + 1) * rows])
        place(1, frame, values[frame * rows:(frame + 1) * rows])
        _, offset = window(frame)
        for half, (first_row, count) in enumerate(parts):
            start = frame * rows + first_row
            some = query[start:start + count]
            some = jnp.concatenate([jnp.where(lane_head == head, some, 0.0) for head in range(heads)], axis=0)
            if offset:
                some = pltpu.roll(some, offset, 1)
            qbd[half][frame] = some.astype(BF16)
    pack(buf.at[p])
    for step in range(2, n_line):
        relay(step, True)
    for load in loads[3:]:
        load.wait()
    for line in range(n_line):
        piece = line * 2 + 1 - b
        kv_copy(own, piece, 2, 0, beside).wait_recv()

    spot = lax.broadcasted_iota(jnp.int32, (1, n_patch * 2 * tail), 1)
    real = (lax.rem(spot, 2 * tail) < tail)

    def spatial(frame, half):
        count = parts[half][1]
        low, offset = window(frame)
        keys = buf[:, 0:main, low:low + wide].reshape(n_patch * main, wide)
        values = buf[:, main:2 * main, low:low + wide].reshape(n_patch * main, wide)
        rest = buf[:, 2 * main:, low:low + wide].reshape(n_patch * 2 * tail, wide)
        query = qbd[half][frame]
        first = lax.dot_general(query, keys, NT, preferred_element_type=F32)
        second = lax.dot_general(query, rest, NT, preferred_element_type=F32)
        second = jnp.where(real, second, -1e30)
        top = jnp.maximum(jnp.max(first, axis=-1, keepdims=True), jnp.max(second, axis=-1, keepdims=True))
        first = jnp.exp((first - top) * scale)
        second = jnp.exp((second - top) * scale)
        norm = jnp.sum(first, axis=-1, keepdims=True) + jnp.sum(second, axis=-1, keepdims=True)
        second = pltpu.roll(second, tail, 1)
        mixed = lax.dot_general(first.astype(BF16), values, NN, preferred_element_type=F32)
        mixed = mixed + lax.dot_general(second.astype(BF16), rest, NN, preferred_element_type=F32)
        mixed = mixed / norm
        total = jnp.zeros((count, wide), F32)
        for head in range(heads):
            start = offset + head * HEAD_DIM
            inside = (lane >= start) & (lane < start + HEAD_DIM)
            total = total + jnp.where(inside, mixed[head * count:(head + 1) * count], 0.0)
        return pltpu.roll(total, wide - offset, 1) if offset else total

    def temporal(half, query, keys, values):
        count = parts[half][1]
        query, keys, values = [x.astype(BF16).astype(F32) for x in (query, keys, values)]
        out = []
        for frame in range(frames):
            one = query[frame * count:(frame + 1) * count]
            products = jnp.concatenate(
                [one * keys[g * count:(g + 1) * count] for g in range(frames)], axis=0)
            products = split_dot(products, group) * scale
            scores = [products[g * count:(g + 1) * count] for g in range(frames)]
            top = functools.reduce(jnp.maximum, scores)
            scores = [jnp.exp(score - top) for score in scores]
            norm = 1.0 / functools.reduce(jnp.add, scores)
            total = jnp.zeros((count, wide), F32)
            for g in range(frames):
                weight = (scores[g] * norm).astype(BF16).astype(F32)
                total = total + weight * values[g * count:(g + 1) * count]
            out.append(total)
        return out

    def middle(half):
        first_row, count = parts[half]
        summed = sum_finish(0, half)
        mine = xg0[t].astype(F32)[first_row:first_row + count]
        value = (mine + mod[2, 0:1] * summed).astype(BF16)
        mid[half][...] = value
        gather_start(1 + half, mid[half], xg1[half])
        xg1[half][t] = value

    def finish(half):
        return mid[half][...].astype(F32) + mod[2, 1:2] * sum_finish(1, half)

    for half in range(n_part):
        attn = []
        for frame in range(frames):
            attn.append(spatial(frame, half))
            if half and frame == frames // 2 - 1:
                sum_across(0, half - 1)
        heads_out(0, half, attn)
        sum_start(0, half)
    middle(0)
    sum_across(0, n_part - 1)
    gather_forward(1, xg1[0])
    for half in range(1, n_part):
        middle(half)
    for half in range(n_part):
        gather_finish(1 + half, xg1[half])
        hmod = modulated(1, xg1[half])
        if half + 1 < n_part:
            gather_forward(2 + half, xg1[half + 1])
        triple = projections(1, hmod)
        if half:
            sum_across(1, half - 1)
        heads_out(1, half, temporal(half, *triple))
        sum_start(1, half)
    sum_across(1, n_part - 1)
    result = [finish(half) for half in range(n_part)]
    out_ref[0] = jnp.concatenate(result, axis=0).astype(BF16)

    for copy in pending:
        copy.wait_send()
    for step in range(n_line):
        relay(step, False)


def local(n_tm, n_patch, stream, stale_keys, stale_values, modulation, w_qkv, w_out, qk_gain):
    frames, rows, width = stale_keys.shape
    depth = stream.shape[2]
    extra = -width % 16
    if extra:
        w_qkv = jnp.pad(w_qkv, ((0, 0), (0, 0), (0, extra), (0, 0)))
        w_out = jnp.pad(w_out, ((0, 0), (0, extra), (0, 0)))
    wide = max((frame * width % 128 + width + 127) // 128 * 128 for frame in range(frames))
    heads = width // HEAD_DIM
    n_chip, n_line = n_tm // 2, n_patch // 2
    cut = (rows // 2 + 15) // 16 * 16
    parts = ((0, cut), (cut, rows - cut))
    n_part = len(parts)
    vmem = pl.BlockSpec(memory_space=pltpu.VMEM)
    hbm = pl.BlockSpec(memory_space=pltpu.HBM)
    far = max(n_chip - 1, 1)

    def each(*lead):
        return [pltpu.VMEM((*lead, count, depth), BF16) for _, count in parts]

    dma = pltpu.SemaphoreType.DMA
    return pl.pallas_call(
        functools.partial(kernel, n_tm, n_patch, width, wide, parts),
        out_shape=jax.ShapeDtypeStruct(stream.shape, BF16),
        in_specs=[hbm] * 7,
        out_specs=vmem,
        scratch_shapes=[
            pltpu.VMEM((2, 3, wide, depth), BF16),
            pltpu.VMEM((2, wide, depth), BF16),
            pltpu.VMEM((2, frames, rows, width), BF16),
            pltpu.VMEM((3, 2, depth), F32),
            pltpu.VMEM((2, 2, HEAD_DIM), F32),
            pltpu.VMEM((2 * rows, frames * width), BF16),
            pltpu.VMEM((n_patch, 2 * rows, frames * width), BF16),
            pltpu.VMEM((2, rows, wide), F32),
            pltpu.VMEM((2, rows, frames * width), F32),
            pltpu.VMEM((frames, rows, depth), BF16),
            *each(frames),
            *each(),
            *[pltpu.VMEM((frames, heads * count, wide), BF16) for _, count in parts],
            *each(frames), *each(frames),
            *each(n_chip), *each(n_chip),
            *each(far), *each(far),
            *each(far), *each(far),
            dma((8,)),
            dma((5,)),
            dma((4, n_line)),
            dma((n_patch,)),
            dma((1 + n_part, n_chip)),
            dma((1 + n_part, n_chip)),
            dma((1 + n_part, n_tm)),
            dma((2 * n_part, n_chip)),
            dma((2 * n_part, n_chip)),
            dma((2 * n_part, far)),
            dma((2 * n_part, far)),
        ],
        compiler_params=pltpu.CompilerParams(
            collective_id=0, has_side_effects=True, vmem_limit_bytes=56 * 1024 * 1024),
        cost_estimate=pl.CostEstimate(flops=4_000_000_000, bytes_accessed=8_000_000, transcendentals=1_000_000),
    )(stream, stale_keys, stale_values, jnp.transpose(modulation, (1, 0, 2)), w_qkv, w_out, qk_gain)


def solution(mesh):
    placed = (
        P("tm", "patch", None),
        P(None, "patch", "tm"),
        P(None, "patch", "tm"),
        P(),
        P(None, None, "tm", None),
        P(None, "tm", None),
        P(),
    )
    return jax.shard_map(
        functools.partial(local, mesh.shape["tm"], mesh.shape["patch"]),
        mesh=mesh, in_specs=placed, out_specs=P("tm", "patch", None), check_vma=False,
    )
```

time: 65.8 us -> 57.6 us (0.88)
  local copies, waits for them, and re-layouts: 8.27 us -> 1.56 us
  Pallas kernels: 57.2 us -> 55.8 us
    unnamed x14 -> x1, local copies, waits for them, and re-layouts: 8.27 us -> 1.56 us
    pallas_call x1, Pallas kernels: 57.2 us -> 55.8 us  [local(): pl.pallas_call(functools.partial(kernel, n_tm, n_patch, width, wide, part...]
where the time goes in v2:
time: 57.6 us; the launch traced here: 57.4 us
  Pallas kernels  55.8 us (97%)
  local copies, waits for them, and re-layouts  1.56 us (3%)
    pallas_call x1, Pallas kernels, local(): pl.pallas_call(functools.partial(kernel, n_tm, n_patch, width, wide, part...  55.8 us
    unnamed x1, local copies, waits for them, and re-layouts  1.56 us

profile of v2, /device:TPU:0, one launch (start us, length us, event | category | flops | bytes accessed | tf_op | source)
XLA Modules:
  0.0 57.4 jit_solution(4078354982088148204)
XLA Ops:
  0.0 55.8 %shard_map.73 = bf16[1,56,1152]{2,1,0:T(8,128)(2,1)} custom-call(bf16[1,56,1152]{2,1,0:T(8,128)(2,1)} %stream_ref.1, bf16[4,56,288]{2,1,0:T(8,128)(2,1)} %old_k_ref.1, bf16[4,56,288]{2,1,0:T(8,128)(2,1)} %old_v_ref.1, f32[3,2,1152]{2,1,0:T(2,128)} %bitcast.1, bf16[2,3,288,1152]{3,2,1,0:T(8,128)(2,1)} %w_qkv_ref.1, bf16[2,288,1152]{2,1,0:T(8,128)(2,1)} %w_out_ref.1, ...), custom_call_target="tpu_custom_call" | custom-call | flops 4000000000 | bytes 8000000 | tf_op jit(solution)/shard_map/pallas_call | solution.py:424
  55.8 1.6 %copy.9 = bf16[1,56,1152]{2,1,0:T(8,128)(2,1)} copy(bf16[1,56,1152]{2,1,0:T(8,128)(2,1)} %shard_map.73) | data formatting | bytes 258048

commit v3 on v2

--- a/solution.py
+++ b/solution.py
@@ -57,6 +57,8 @@
     tail = rows - main
     n_chip = n_tm // 2
     n_line = n_patch // 2
+    upper = rows // 16 * 16
+    cuts = ((0, upper), (upper, 2 * rows - upper))
     scale = HEAD_DIM ** (-0.5)
 
     t = lax.axis_index("tm")
@@ -141,34 +143,91 @@
         copy.start()
         pending.append(copy)
 
-    def kv_copy(src, piece, kind, step, where):
-        return remote(src, buf.at[piece], kv_send.at[kind, step], kv_recv.at[piece], {"patch": where})
-
-    def relay(step, go):
+    def kv_copy(src, line, side, cut, kind, step, **where):
+        first, count = cuts[cut]
+        rows_of = pl.ds(first, count)
+        return remote(src.at[rows_of], buf.at[side, line, rows_of], kv_send.at[kind, step, cut],
+                      kv_recv.at[side, line, cut], where)
+
+    def kv_arrived(line, side, cut):
+        kv_copy(own, line, side, cut, 0, 0, patch=beside).wait_recv()
+
+    def move(copy, go):
+        copy.start() if go else copy.wait_send()
+
+    def spot_on_line(line):
+        return jnp.clip(line, 0, n_line - 1)
+
+    even = n_line == 4
+    at_end = (a == 0) | (a == n_line - 1)
+    inward = jnp.where(a == 0, 1, a - 1)
+    outward = jnp.where(a == 1, 0, n_line - 1)
+    far_end = jnp.where(a == 1, n_line - 1, 0)
+
+    def relay(step, cut, go):
         for kind, sign in ((0, 1), (1, -1)):
             origin = a - sign * step
             onward = a + sign
-            piece = jnp.clip(origin, 0, n_line - 1) * 2 + b
-            src = own if step == 0 else buf.at[piece]
+            line = spot_on_line(origin)
+            src = buf.at[b, line] if step else own
             here = (origin >= 0) & (origin < n_line)
 
-            @pl.when(here)
-            def _():
-                if step and go:
-                    kv_copy(src, piece, kind, step, beside).wait_recv()
-                if step:
-                    across = kv_copy(src, piece, 2 + kind, step, beside)
-                    across.start() if go else across.wait_send()
+            if step:
+                @pl.when(here)
+                def _():
+                    if go:
+                        kv_arrived(line, b, cut)
+
+                across = here
+                if even and step == 1:
+                    across = here & (origin != 0) & (origin != n_line - 1)
+                if even and step == n_line - 1 and cut == 1:
+                    across = None
+                if across is not None:
+                    @pl.when(across)
+                    def _():
+                        move(kv_copy(src, line, b, cut, 2 + kind, step, patch=beside), go)
 
             @pl.when(here & (onward >= 0) & (onward < n_line))
             def _():
-                along = kv_copy(src, piece, kind, step, jnp.clip(onward, 0, n_line - 1) * 2 + b)
-                along.start() if go else along.wait_send()
+                move(kv_copy(src, line, b, cut, kind, step, patch=spot_on_line(onward) * 2 + b), go)
         if step == 0:
-            across = kv_copy(own, p, 2, 0, beside)
-            across.start() if go else across.wait_send()
-
-    relay(0, True)
+            move(kv_copy(own, a, b, cut, 2, 0, patch=beside), go)
+
+    def relay_end(cut, go):
+        if even:
+            @pl.when(at_end)
+            def _():
+                if go:
+                    kv_arrived(a, 1 - b, cut)
+                move(kv_copy(buf.at[1 - b, a], a, 1 - b, cut, 4, 0, patch=inward * 2 + b), go)
+
+    def relay_far(go):
+        if even:
+            @pl.when(jnp.logical_not(at_end))
+            def _():
+                if go:
+                    kv_arrived(far_end, 1 - b, 1)
+                move(kv_copy(buf.at[1 - b, far_end], far_end, 1 - b, 1, 4, 1, patch=outward * 2 + b), go)
+
+    def final_waits():
+        for line in range(n_line):
+            for cut in range(2):
+                forwarded = False
+                if even and line in (0, n_line - 1):
+                    forwarded = at_end & (a == line)
+                    if cut == 1:
+                        forwarded = forwarded | (jnp.logical_not(at_end) & (far_end == line))
+
+                if forwarded is False:
+                    kv_arrived(line, 1 - b, cut)
+                else:
+                    @pl.when(jnp.logical_not(forwarded))
+                    def _():
+                        kv_arrived(line, 1 - b, cut)
+
+    for cut in range(2):
+        relay(0, cut, True)
 
     def gather_start(phase, src, xg):
         for j in range(1, n_chip):
@@ -279,13 +338,19 @@
         return total
 
     gather_forward(0, xg0)
+    if n_line > 1:
+        relay(1, 0, True)
+        relay_end(0, True)
     gather_finish(0, xg0)
     hmod = modulated(0, xg0)
     if n_line > 1:
-        relay(1, True)
+        relay(1, 1, True)
+        relay_end(1, True)
     for load in loads[:3]:
         load.wait()
     query, keys, values = projections(0, hmod)
+    if n_line > 2:
+        relay(2, 0, True)
     acc[...] = jnp.zeros_like(acc)
     for frame in range(frames):
         place(0, frame, keys[frame * rows:(frame + 1) * rows])
@@ -298,14 +363,15 @@
             if offset:
                 some = pltpu.roll(some, offset, 1)
             qbd[half][frame] = some.astype(BF16)
-    pack(buf.at[p])
+    pack(buf.at[b, a])
     for step in range(2, n_line):
-        relay(step, True)
+        for cut in range(2):
+            if (step, cut) != (2, 0):
+                relay(step, cut, True)
+    relay_far(True)
     for load in loads[3:]:
         load.wait()
-    for line in range(n_line):
-        piece = line * 2 + 1 - b
-        kv_copy(own, piece, 2, 0, beside).wait_recv()
+    final_waits()
 
     spot = lax.broadcasted_iota(jnp.int32, (1, n_patch * 2 * tail), 1)
     real = (lax.rem(spot, 2 * tail) < tail)
@@ -313,9 +379,9 @@
     def spatial(frame, half):
         count = parts[half][1]
         low, offset = window(frame)
-        keys = buf[:, 0:main, low:low + wide].reshape(n_patch * main, wide)
-        values = buf[:, main:2 * main, low:low + wide].reshape(n_patch * main, wide)
-        rest = buf[:, 2 * main:, low:low + wide].reshape(n_patch * 2 * tail, wide)
+        keys = buf[:, :, 0:main, low:low + wide].reshape(n_patch * main, wide)
+        values = buf[:, :, main:2 * main, low:low + wide].reshape(n_patch * main, wide)
+        rest = buf[:, :, 2 * main:, low:low + wide].reshape(n_patch * 2 * tail, wide)
         query = qbd[half][frame]
         first = lax.dot_general(query, keys, NT, preferred_element_type=F32)
         second = lax.dot_general(query, rest, NT, preferred_element_type=F32)
@@ -397,7 +463,11 @@
     for copy in pending:
         copy.wait_send()
     for step in range(n_line):
-        relay(step, False)
+        for cut in range(2):
+            relay(step, cut, False)
+    for cut in range(2):
+        relay_end(cut, False)
+    relay_far(False)
 
 
 def local(n_tm, n_patch, stream, stale_keys, stale_values, modulation, w_qkv, w_out, qk_gain):
@@ -433,7 +503,7 @@
             pltpu.VMEM((3, 2, depth), F32),
             pltpu.VMEM((2, 2, HEAD_DIM), F32),
             pltpu.VMEM((2 * rows, frames * width), BF16),
-            pltpu.VMEM((n_patch, 2 * rows, frames * width), BF16),
+            pltpu.VMEM((2, n_line, 2 * rows, frames * width), BF16),
             pltpu.VMEM((2, rows, wide), F32),
             pltpu.VMEM((2, rows, frames * width), F32),
             pltpu.VMEM((frames, rows, depth), BF16),
@@ -446,8 +516,8 @@
             *each(far), *each(far),
             dma((8,)),
             dma((5,)),
-            dma((4, n_line)),
-            dma((n_patch,)),
+            dma((5, max(n_line, 2), 2)),
+            dma((2, n_line, 2)),
             dma((1 + n_part, n_chip)),
             dma((1 + n_part, n_chip)),
             dma((1 + n_part, n_tm)),

time: 57.6 us -> 53.8 us (0.934)
  Pallas kernels: 55.8 us -> 52.1 us
    pallas_call x1, Pallas kernels: 55.8 us -> 52.1 us  [local(): pl.pallas_call(functools.partial(kernel, n_tm, n_patch, width, wide, part...]
where the time goes in v3:
time: 53.8 us; the launch traced here: 53.7 us
  Pallas kernels  52.1 us (97%)
  local copies, waits for them, and re-layouts  1.56 us (3%)
    pallas_call x1, Pallas kernels, local(): pl.pallas_call(functools.partial(kernel, n_tm, n_patch, width, wide, part...  52.1 us
    unnamed x1, local copies, waits for them, and re-layouts  1.56 us

profile of v3, /device:TPU:0, one launch (start us, length us, event | category | flops | bytes accessed | tf_op | source)
XLA Modules:
  0.0 53.7 jit_solution(14958892942441475655)
XLA Ops:
  0.0 52.1 %shard_map.73 = bf16[1,56,1152]{2,1,0:T(8,128)(2,1)} custom-call(bf16[1,56,1152]{2,1,0:T(8,128)(2,1)} %stream_ref.1, bf16[4,56,288]{2,1,0:T(8,128)(2,1)} %old_k_ref.1, bf16[4,56,288]{2,1,0:T(8,128)(2,1)} %old_v_ref.1, f32[3,2,1152]{2,1,0:T(2,128)} %bitcast.1, bf16[2,3,288,1152]{3,2,1,0:T(8,128)(2,1)} %w_qkv_ref.1, bf16[2,288,1152]{2,1,0:T(8,128)(2,1)} %w_out_ref.1, ...), custom_call_target="tpu_custom_call" | custom-call | flops 4000000000 | bytes 8000000 | tf_op jit(solution)/shard_map/pallas_call | solution.py:494
  52.1 1.6 %copy.9 = bf16[1,56,1152]{2,1,0:T(8,128)(2,1)} copy(bf16[1,56,1152]{2,1,0:T(8,128)(2,1)} %shard_map.73) | data formatting | bytes 258048

commit v4 on v3

--- a/solution.py
+++ b/solution.py
@@ -43,7 +43,7 @@
     def take():
         return [rest_refs.pop(0) for _ in range(n_part)]
 
-    xg1, mid, qbd = take(), take(), take()
+    xg1, chip_sum, all_sum, qbd = take(), take(), take(), take()
     partial = [take(), take()]
     rp, sx, rx = [take(), take()], [take(), take()], [take(), take()]
     (w_sem, in_sem, kv_send, kv_recv, ag_send_x, ag_send_p, ag_recv,
@@ -121,14 +121,16 @@
             value = pltpu.roll(value, offset, 1)
         acc[which, :, low:low + wide] += value
 
-    acc[...] = jnp.zeros_like(acc)
-    stage[...] = jnp.zeros_like(stage)
-    for which in range(2):
+    def stale(which):
         inputs[which].wait()
         for frame in range(frames):
             stage[which, :, 0:width] = old[which, frame].astype(F32)
             place(which, frame, stage[which])
-    pack(own)
+
+    acc[...] = jnp.zeros_like(acc)
+    stage[...] = jnp.zeros_like(stage)
+    stale(0)
+    own[0:main] = acc[0, 0:main].astype(BF16)
 
     met = 1 + n_chip + jnp.where(a > 0, 1, 0) + jnp.where(a < n_line - 1, 1, 0)
     pl.semaphore_wait(barrier, met)
@@ -181,6 +183,8 @@
                 across = here
                 if even and step == 1:
                     across = here & (origin != 0) & (origin != n_line - 1)
+                if even and step == 2:
+                    across = here & at_end
                 if even and step == n_line - 1 and cut == 1:
                     across = None
                 if across is not None:
@@ -193,6 +197,13 @@
                 move(kv_copy(src, line, b, cut, kind, step, patch=spot_on_line(onward) * 2 + b), go)
         if step == 0:
             move(kv_copy(own, a, b, cut, 2, 0, patch=beside), go)
+
+    def relay_across(go):
+        if even:
+            @pl.when(jnp.logical_not(at_end))
+            def _():
+                for cut in (1, 0):
+                    move(kv_copy(buf.at[b, far_end], far_end, b, cut, 2, 2, patch=beside), go)
 
     def relay_end(cut, go):
         if even:
@@ -226,9 +237,6 @@
                     def _():
                         kv_arrived(line, 1 - b, cut)
 
-    for cut in range(2):
-        relay(0, cut, True)
-
     def gather_start(phase, src, xg):
         for j in range(1, n_chip):
             started(remote(src, xg.at[t], ag_send_x.at[phase, j], ag_recv.at[phase, t],
@@ -250,8 +258,12 @@
         for j in range(n_chip):
             gather_arrived(phase, xg, other_chip(j) * 2 + 1 - core)
 
+    relay(0, 0, True)
     inputs[2].wait()
     gather_start(0, xg0.at[t], xg0)
+    stale(1)
+    own[main:] = jnp.concatenate([acc[1, 0:main], acc[0, main:], acc[1, main:]], axis=0).astype(BF16)
+    relay(0, 1, True)
 
     features = lax.broadcasted_iota(jnp.int32, (wide, wide), 0)
     columns = lax.broadcasted_iota(jnp.int32, (wide, wide), 1)
@@ -326,6 +338,31 @@
             outbox[j - 1] = (part[to * 2 + core].astype(F32) + inbox[to].astype(F32)).astype(BF16)
             started(remote(outbox.at[j - 1], rx[block][half].at[j - 1], rs_send_x.at[phase, j - 1],
                            rs_recv_x.at[phase, j - 1], {"tm": to * 2 + core}))
+
+    def all_across(half):
+        part, inbox, outbox = partial[0][half], rp[0][half], chip_sum[half]
+        for j in range(n_chip):
+            to = other_chip(j)
+            sum_arrived(half, inbox, to)
+            outbox[to] = (part[to * 2 + core].astype(F32) + inbox[to].astype(F32)).astype(BF16)
+        for j in range(1, n_chip):
+            started(remote(outbox, all_sum[half].at[j - 1], rs_send_x.at[half, j - 1],
+                           rs_recv_x.at[half, j - 1], {"tm": other_chip(j) * 2 + core}))
+
+    def middle(half):
+        first_row, count = parts[half]
+        for j in range(1, n_chip):
+            remote(chip_sum[half], all_sum[half].at[j - 1], rs_send_x.at[half, j - 1],
+                   rs_recv_x.at[half, j - 1], {"tm": partner}).wait_recv()
+        for c in range(n_chip):
+            frame = c * 2 + core
+            total = chip_sum[half][c].astype(F32)
+            for j in range(1, n_chip):
+                total = total + all_sum[half][j - 1, c].astype(F32)
+            mine = xg0[frame].astype(F32)[first_row:first_row + count]
+            xg1[half][frame] = (mine + mod[2, 0:1] * total).astype(BF16)
+            started(remote(xg1[half].at[frame], xg1[half].at[frame], ag_send_p.at[1 + half, c],
+                           ag_recv.at[1 + half, frame], {"tm": partner}))
 
     def sum_finish(block, half):
         phase = block * n_part + half
@@ -368,6 +405,8 @@
         for cut in range(2):
             if (step, cut) != (2, 0):
                 relay(step, cut, True)
+        if step == 2:
+            relay_across(True)
     relay_far(True)
     for load in loads[3:]:
         load.wait()
@@ -421,36 +460,24 @@
             out.append(total)
         return out
 
-    def middle(half):
-        first_row, count = parts[half]
-        summed = sum_finish(0, half)
-        mine = xg0[t].astype(F32)[first_row:first_row + count]
-        value = (mine + mod[2, 0:1] * summed).astype(BF16)
-        mid[half][...] = value
-        gather_start(1 + half, mid[half], xg1[half])
-        xg1[half][t] = value
-
     def finish(half):
-        return mid[half][...].astype(F32) + mod[2, 1:2] * sum_finish(1, half)
+        return xg1[half][t].astype(F32) + mod[2, 1:2] * sum_finish(1, half)
 
     for half in range(n_part):
         attn = []
         for frame in range(frames):
             attn.append(spatial(frame, half))
             if half and frame == frames // 2 - 1:
-                sum_across(0, half - 1)
+                all_across(half - 1)
         heads_out(0, half, attn)
         sum_start(0, half)
     middle(0)
-    sum_across(0, n_part - 1)
-    gather_forward(1, xg1[0])
-    for half in range(1, n_part):
-        middle(half)
+    all_across(n_part - 1)
     for half in range(n_part):
         gather_finish(1 + half, xg1[half])
         hmod = modulated(1, xg1[half])
         if half + 1 < n_part:
-            gather_forward(2 + half, xg1[half + 1])
+            middle(half + 1)
         triple = projections(1, hmod)
         if half:
             sum_across(1, half - 1)
@@ -467,6 +494,7 @@
             relay(step, cut, False)
     for cut in range(2):
         relay_end(cut, False)
+    relay_across(False)
     relay_far(False)
 
 
@@ -508,7 +536,8 @@
             pltpu.VMEM((2, rows, frames * width), F32),
             pltpu.VMEM((frames, rows, depth), BF16),
             *each(frames),
-            *each(),
+            *each(n_chip),
+            *each(far, n_chip),
             *[pltpu.VMEM((frames, heads * count, wide), BF16) for _, count in parts],
             *each(frames), *each(frames),
             *each(n_chip), *each(n_chip),

time: 53.8 us -> 52.2 us (0.970)
  Pallas kernels: 52.1 us -> 50.5 us
    pallas_call x1, Pallas kernels: 52.1 us -> 50.5 us  [local(): pl.pallas_call(functools.partial(kernel, n_tm, n_patch, width, wide, part...]
where the time goes in v4:
time: 52.2 us; the launch traced here: 52.1 us
  Pallas kernels  50.5 us (97%)
  local copies, waits for them, and re-layouts  1.56 us (3%)
    pallas_call x1, Pallas kernels, local(): pl.pallas_call(functools.partial(kernel, n_tm, n_patch, width, wide, part...  50.5 us
    unnamed x1, local copies, waits for them, and re-layouts  1.56 us

profile of v4, /device:TPU:0, one launch (start us, length us, event | category | flops | bytes accessed | tf_op | source)
XLA Modules:
  0.0 52.1 jit_solution(11132345821429826946)
XLA Ops:
  0.0 50.5 %shard_map.73 = bf16[1,56,1152]{2,1,0:T(8,128)(2,1)} custom-call(bf16[1,56,1152]{2,1,0:T(8,128)(2,1)} %stream_ref.1, bf16[4,56,288]{2,1,0:T(8,128)(2,1)} %old_k_ref.1, bf16[4,56,288]{2,1,0:T(8,128)(2,1)} %old_v_ref.1, f32[3,2,1152]{2,1,0:T(2,128)} %bitcast.1, bf16[2,3,288,1152]{3,2,1,0:T(8,128)(2,1)} %w_qkv_ref.1, bf16[2,288,1152]{2,1,0:T(8,128)(2,1)} %w_out_ref.1, ...), custom_call_target="tpu_custom_call" | custom-call | flops 4000000000 | bytes 8000000 | tf_op jit(solution)/shard_map/pallas_call | solution.py:522
  50.5 1.6 %copy.9 = bf16[1,56,1152]{2,1,0:T(8,128)(2,1)} copy(bf16[1,56,1152]{2,1,0:T(8,128)(2,1)} %shard_map.73) | data formatting | bytes 258048

commit v5 on v4

--- a/solution.py
+++ b/solution.py
@@ -43,7 +43,7 @@
     def take():
         return [rest_refs.pop(0) for _ in range(n_part)]
 
-    xg1, chip_sum, all_sum, qbd = take(), take(), take(), take()
+    xg1, chip_sum, all_sum, qbd, early = take(), take(), take(), take(), take()
     partial = [take(), take()]
     rp, sx, rx = [take(), take()], [take(), take()], [take(), take()]
     (w_sem, in_sem, kv_send, kv_recv, ag_send_x, ag_send_p, ag_recv,
@@ -408,36 +408,52 @@
         if step == 2:
             relay_across(True)
     relay_far(True)
+
+    spot = lax.broadcasted_iota(jnp.int32, (1, n_line * rows + n_line * tail), 1)
+    in_main = spot < n_line * main
+    in_tail = lax.rem(spot, 2 * tail) < tail
+    if n_line * main % (2 * tail):
+        in_tail = lax.rem(jnp.maximum(spot - n_line * main, 0), 2 * tail) < tail
+
+    def column_attention(frame, half, side):
+        count = parts[half][1]
+        low, offset = window(frame)
+        rest = buf[side, :, 2 * main:, low:low + wide].reshape(n_line * 2 * tail, wide)
+        keys = buf[side, :, 0:main, low:low + wide].reshape(n_line * main, wide)
+        values = buf[side, :, main:2 * main, low:low + wide].reshape(n_line * main, wide)
+        keys = jnp.concatenate([keys, rest], axis=0)
+        values = jnp.concatenate([values, rest], axis=0)
+        scores = lax.dot_general(qbd[half][frame], keys, NT, preferred_element_type=F32)
+        scores = jnp.where(in_main | in_tail, scores, -1e30)
+        top = jnp.max(scores, axis=-1, keepdims=True)
+        weights = jnp.exp((scores - top) * scale)
+        norm = jnp.sum(weights, axis=-1, keepdims=True)
+        moved = jnp.where(in_tail, 0.0, pltpu.roll(weights, tail, 1))
+        weights = jnp.where(in_main, weights, moved).astype(BF16)
+        mixed = lax.dot_general(weights, values, NN, preferred_element_type=F32)
+        out = [jnp.zeros((count, wide), F32), jnp.zeros((count, wide), F32), jnp.ones((count, wide), F32)]
+        for head in range(heads):
+            start = offset + head * HEAD_DIM
+            inside = (lane >= start) & (lane < start + HEAD_DIM)
+            of_head = slice(head * count, (head + 1) * count)
+            out = [jnp.where(inside, x[of_head], y) for x, y in zip((mixed, top, norm), out)]
+        return out
+
+    for half in range(n_part):
+        for frame in range(frames):
+            for i, value in enumerate(column_attention(frame, half, b)):
+                early[half][i, frame] = value
     for load in loads[3:]:
         load.wait()
     final_waits()
 
-    spot = lax.broadcasted_iota(jnp.int32, (1, n_patch * 2 * tail), 1)
-    real = (lax.rem(spot, 2 * tail) < tail)
-
     def spatial(frame, half):
-        count = parts[half][1]
-        low, offset = window(frame)
-        keys = buf[:, :, 0:main, low:low + wide].reshape(n_patch * main, wide)
-        values = buf[:, :, main:2 * main, low:low + wide].reshape(n_patch * main, wide)
-        rest = buf[:, :, 2 * main:, low:low + wide].reshape(n_patch * 2 * tail, wide)
-        query = qbd[half][frame]
-        first = lax.dot_general(query, keys, NT, preferred_element_type=F32)
-        second = lax.dot_general(query, rest, NT, preferred_element_type=F32)
-        second = jnp.where(real, second, -1e30)
-        top = jnp.maximum(jnp.max(first, axis=-1, keepdims=True), jnp.max(second, axis=-1, keepdims=True))
-        first = jnp.exp((first - top) * scale)
-        second = jnp.exp((second - top) * scale)
-        norm = jnp.sum(first, axis=-1, keepdims=True) + jnp.sum(second, axis=-1, keepdims=True)
-        second = pltpu.roll(second, tail, 1)
-        mixed = lax.dot_general(first.astype(BF16), values, NN, preferred_element_type=F32)
-        mixed = mixed + lax.dot_general(second.astype(BF16), rest, NN, preferred_element_type=F32)
-        mixed = mixed / norm
-        total = jnp.zeros((count, wide), F32)
-        for head in range(heads):
-            start = offset + head * HEAD_DIM
-            inside = (lane >= start) & (lane < start + HEAD_DIM)
-            total = total + jnp.where(inside, mixed[head * count:(head + 1) * count], 0.0)
+        weighted, top, norm = column_attention(frame, half, 1 - b)
+        before, top_before, norm_before = [early[half][i, frame] for i in range(3)]
+        highest = jnp.maximum(top, top_before)
+        now, then = jnp.exp((top - highest) * scale), jnp.exp((top_before - highest) * scale)
+        total = (weighted * now + before * then) / (norm * now + norm_before * then)
+        _, offset = window(frame)
         return pltpu.roll(total, wide - offset, 1) if offset else total
 
     def temporal(half, query, keys, values):
@@ -539,6 +555,7 @@
             *each(n_chip),
             *each(far, n_chip),
             *[pltpu.VMEM((frames, heads * count, wide), BF16) for _, count in parts],
+            *[pltpu.VMEM((3, frames, count, wide), F32) for _, count in parts],
             *each(frames), *each(frames),
             *each(n_chip), *each(n_chip),
             *each(far), *each(far),

time: 52.2 us -> 52.1 us (level)
  no operation moved by 1% of the time
where the time goes in v5:
time: 52.1 us; the launch traced here: 52 us
  Pallas kernels  50.4 us (97%)
  local copies, waits for them, and re-layouts  1.56 us (3%)
    pallas_call x1, Pallas kernels, local(): pl.pallas_call(functools.partial(kernel, n_tm, n_patch, width, wide, part...  50.4 us
    unnamed x1, local copies, waits for them, and re-layouts  1.56 us

profile of v5, /device:TPU:0, one launch (start us, length us, event | category | flops | bytes accessed | tf_op | source)
XLA Modules:
  0.0 52.0 jit_solution(4817536623064829080)
XLA Ops:
  0.0 50.4 %shard_map.73 = bf16[1,56,1152]{2,1,0:T(8,128)(2,1)} custom-call(bf16[1,56,1152]{2,1,0:T(8,128)(2,1)} %stream_ref.1, bf16[4,56,288]{2,1,0:T(8,128)(2,1)} %old_k_ref.1, bf16[4,56,288]{2,1,0:T(8,128)(2,1)} %old_v_ref.1, f32[3,2,1152]{2,1,0:T(2,128)} %bitcast.1, bf16[2,3,288,1152]{3,2,1,0:T(8,128)(2,1)} %w_qkv_ref.1, bf16[2,288,1152]{2,1,0:T(8,128)(2,1)} %w_out_ref.1, ...), custom_call_target="tpu_custom_call" | custom-call | flops 4000000000 | bytes 8000000 | tf_op jit(solution)/shard_map/pallas_call | solution.py:538
  50.4 1.6 %copy.9 = bf16[1,56,1152]{2,1,0:T(8,128)(2,1)} copy(bf16[1,56,1152]{2,1,0:T(8,128)(2,1)} %shard_map.73) | data formatting | bytes 258048

commit v6 on v5

--- a/solution.py
+++ b/solution.py
@@ -26,6 +26,10 @@
 def split_dot(left, right):
     high = left.astype(BF16)
     low = (left - high.astype(F32)).astype(BF16)
+    count = left.shape[0]
+    if count % 16 == 0:
+        both = lax.dot_general(jnp.concatenate([high, low], axis=0), right, NN, preferred_element_type=F32)
+        return both[:count] + both[count:]
     return lax.dot_general(high, right, NN, preferred_element_type=F32) + lax.dot_general(
         low, right, NN, preferred_element_type=F32
     )
@@ -291,24 +295,20 @@
 
     def modulated(block, xg):
         shift, gain = mod[0, block:block + 1], 1.0 + mod[1, block:block + 1]
-        out = []
-        for frame in range(frames):
-            values = xg[frame].astype(F32)
-            center = jnp.mean(values, axis=-1, keepdims=True)
-            values = values - center
-            spread_ = jnp.mean(values * values, axis=-1, keepdims=True)
-            out.append(values * lax.rsqrt(spread_ + EPS) * gain + shift)
-        return jnp.concatenate(out, axis=0).astype(BF16)
+        values = jnp.concatenate([xg[frame].astype(F32) for frame in range(frames)], axis=0)
+        center = jnp.mean(values, axis=-1, keepdims=True)
+        values = values - center
+        spread_ = jnp.mean(values * values, axis=-1, keepdims=True)
+        return (values * lax.rsqrt(spread_ + EPS) * gain + shift).astype(BF16)
 
     def projections(block, hmod):
         raw = lax.dot_general(
             hmod, wq[block].reshape(3 * wide, depth), NT, preferred_element_type=F32)
-        out = []
-        for c in range(2):
-            piece = raw[:, c * wide:(c + 1) * wide]
-            square = split_dot(piece * piece, group) * (1.0 / HEAD_DIM)
-            out.append(piece * lax.rsqrt(square + EPS) * gain_rows[block][c])
-        return out + [raw[:, 2 * wide:]]
+        count = raw.shape[0]
+        two = jnp.concatenate([raw[:, :wide], raw[:, wide:2 * wide]], axis=0)
+        square = split_dot(two * two, group) * (1.0 / HEAD_DIM)
+        two = two * lax.rsqrt(square + EPS)
+        return [two[:count] * gain_rows[block][0], two[count:] * gain_rows[block][1], raw[:, 2 * wide:]]
 
     def heads_out(block, half, attn):
         count = parts[half][1]
@@ -415,65 +415,85 @@
     if n_line * main % (2 * tail):
         in_tail = lax.rem(jnp.maximum(spot - n_line * main, 0), 2 * tail) < tail
 
-    def column_attention(frame, half, side):
-        count = parts[half][1]
-        low, offset = window(frame)
-        rest = buf[side, :, 2 * main:, low:low + wide].reshape(n_line * 2 * tail, wide)
-        keys = buf[side, :, 0:main, low:low + wide].reshape(n_line * main, wide)
-        values = buf[side, :, main:2 * main, low:low + wide].reshape(n_line * main, wide)
-        keys = jnp.concatenate([keys, rest], axis=0)
-        values = jnp.concatenate([values, rest], axis=0)
-        scores = lax.dot_general(qbd[half][frame], keys, NT, preferred_element_type=F32)
+    def column_attention(halves, some, side):
+        scores, values = [], []
+        for frame in some:
+            low, _ = window(frame)
+            rest = buf[side, :, 2 * main:, low:low + wide].reshape(n_line * 2 * tail, wide)
+            keys = buf[side, :, 0:main, low:low + wide].reshape(n_line * main, wide)
+            value = buf[side, :, main:2 * main, low:low + wide].reshape(n_line * main, wide)
+            keys = jnp.concatenate([keys, rest], axis=0)
+            values.append(jnp.concatenate([value, rest], axis=0))
+            query = jnp.concatenate([qbd[half][frame] for half in halves], axis=0)
+            scores.append(lax.dot_general(query, keys, NT, preferred_element_type=F32))
+        size = scores[0].shape[0]
+        scores = jnp.concatenate(scores, axis=0)
         scores = jnp.where(in_main | in_tail, scores, -1e30)
         top = jnp.max(scores, axis=-1, keepdims=True)
         weights = jnp.exp((scores - top) * scale)
         norm = jnp.sum(weights, axis=-1, keepdims=True)
         moved = jnp.where(in_tail, 0.0, pltpu.roll(weights, tail, 1))
-        weights = jnp.where(in_main, weights, moved).astype(BF16)
-        mixed = lax.dot_general(weights, values, NN, preferred_element_type=F32)
-        out = [jnp.zeros((count, wide), F32), jnp.zeros((count, wide), F32), jnp.ones((count, wide), F32)]
-        for head in range(heads):
-            start = offset + head * HEAD_DIM
-            inside = (lane >= start) & (lane < start + HEAD_DIM)
-            of_head = slice(head * count, (head + 1) * count)
-            out = [jnp.where(inside, x[of_head], y) for x, y in zip((mixed, top, norm), out)]
-        return out
-
-    for half in range(n_part):
-        for frame in range(frames):
-            for i, value in enumerate(column_attention(frame, half, b)):
-                early[half][i, frame] = value
+        weights = jnp.where(in_main, weights, moved)
+        mixed = [
+            lax.dot_general(weights[i * size:(i + 1) * size].astype(BF16), values[i], NN, preferred_element_type=F32)
+            for i in range(len(some))]
+        done = []
+        for i, frame in enumerate(some):
+            _, offset = window(frame)
+            begin = 0
+            for half in halves:
+                count = parts[half][1]
+                out = [jnp.zeros((count, wide), F32), jnp.zeros((count, wide), F32), jnp.ones((count, wide), F32)]
+                for head in range(heads):
+                    start = offset + head * HEAD_DIM
+                    inside = (lane >= start) & (lane < start + HEAD_DIM)
+                    here, there = slice(begin, begin + count), slice(i * size + begin, i * size + begin + count)
+                    out = [jnp.where(inside, x, y)
+                           for x, y in zip((mixed[i][here], top[there], norm[there]), out)]
+                    begin += count
+                done.append((half, frame, out))
+        return done
+
+    batches = [list(range(frames))[i:i + 4] for i in range(0, frames, 4)]
+    for some in batches:
+        for half, frame, out in column_attention(range(n_part), some, b):
+            for i in range(3):
+                early[half][i, frame] = out[i]
     for load in loads[3:]:
         load.wait()
     final_waits()
 
-    def spatial(frame, half):
-        weighted, top, norm = column_attention(frame, half, 1 - b)
-        before, top_before, norm_before = [early[half][i, frame] for i in range(3)]
-        highest = jnp.maximum(top, top_before)
-        now, then = jnp.exp((top - highest) * scale), jnp.exp((top_before - highest) * scale)
-        total = (weighted * now + before * then) / (norm * now + norm_before * then)
-        _, offset = window(frame)
-        return pltpu.roll(total, wide - offset, 1) if offset else total
+    def spatial(some, half):
+        result = []
+        for _, frame, (weighted, top, norm) in column_attention([half], some, 1 - b):
+            before, top_before, norm_before = [early[half][i, frame] for i in range(3)]
+            highest = jnp.maximum(top, top_before)
+            now, then = jnp.exp((top - highest) * scale), jnp.exp((top_before - highest) * scale)
+            total = (weighted * now + before * then) / (norm * now + norm_before * then)
+            _, offset = window(frame)
+            result.append(pltpu.roll(total, wide - offset, 1) if offset else total)
+        return result
 
     def temporal(half, query, keys, values):
         count = parts[half][1]
         query, keys, values = [x.astype(BF16).astype(F32) for x in (query, keys, values)]
         out = []
-        for frame in range(frames):
-            one = query[frame * count:(frame + 1) * count]
+        some = max(1, 16 // frames)
+        for begin in range(0, frames, some):
+            ones = [query[f * count:(f + 1) * count] for f in range(begin, min(begin + some, frames))]
             products = jnp.concatenate(
-                [one * keys[g * count:(g + 1) * count] for g in range(frames)], axis=0)
+                [one * keys[g * count:(g + 1) * count] for one in ones for g in range(frames)], axis=0)
             products = split_dot(products, group) * scale
-            scores = [products[g * count:(g + 1) * count] for g in range(frames)]
-            top = functools.reduce(jnp.maximum, scores)
-            scores = [jnp.exp(score - top) for score in scores]
-            norm = 1.0 / functools.reduce(jnp.add, scores)
-            total = jnp.zeros((count, wide), F32)
-            for g in range(frames):
-                weight = (scores[g] * norm).astype(BF16).astype(F32)
-                total = total + weight * values[g * count:(g + 1) * count]
-            out.append(total)
+            for i in range(len(ones)):
+                scores = [products[(i * frames + g) * count:(i * frames + g + 1) * count] for g in range(frames)]
+                top = functools.reduce(jnp.maximum, scores)
+                scores = [jnp.exp(score - top) for score in scores]
+                norm = 1.0 / functools.reduce(jnp.add, scores)
+                total = jnp.zeros((count, wide), F32)
+                for g in range(frames):
+                    weight = (scores[g] * norm).astype(BF16).astype(F32)
+                    total = total + weight * values[g * count:(g + 1) * count]
+                out.append(total)
         return out
 
     def finish(half):
@@ -481,10 +501,10 @@
 
     for half in range(n_part):
         attn = []
-        for frame in range(frames):
-            attn.append(spatial(frame, half))
-            if half and frame == frames // 2 - 1:
-                all_across(half - 1)
+        for some in batches:
+            attn += spatial(some, half)
+        if half:
+            all_across(half - 1)
         heads_out(0, half, attn)
         sum_start(0, half)
     middle(0)

time: 52.1 us -> 51.4 us (0.987)
  Pallas kernels: 50.4 us -> 49.7 us
    pallas_call x1, Pallas kernels: 50.4 us -> 49.7 us  [local(): pl.pallas_call(functools.partial(kernel, n_tm, n_patch, width, wide, part...]
where the time goes in v6:
time: 51.4 us; the launch traced here: 51.2 us
  Pallas kernels  49.7 us (97%)
  local copies, waits for them, and re-layouts  1.56 us (3%)
    pallas_call x1, Pallas kernels, local(): pl.pallas_call(functools.partial(kernel, n_tm, n_patch, width, wide, part...  49.7 us
    unnamed x1, local copies, waits for them, and re-layouts  1.56 us

profile of v6, /device:TPU:0, one launch (start us, length us, event | category | flops | bytes accessed | tf_op | source)
XLA Modules:
  0.0 51.2 jit_solution(14352398765719579576)
XLA Ops:
  0.0 49.7 %shard_map.73 = bf16[1,56,1152]{2,1,0:T(8,128)(2,1)} custom-call(bf16[1,56,1152]{2,1,0:T(8,128)(2,1)} %stream_ref.1, bf16[4,56,288]{2,1,0:T(8,128)(2,1)} %old_k_ref.1, bf16[4,56,288]{2,1,0:T(8,128)(2,1)} %old_v_ref.1, f32[3,2,1152]{2,1,0:T(2,128)} %bitcast.1, bf16[2,3,288,1152]{3,2,1,0:T(8,128)(2,1)} %w_qkv_ref.1, bf16[2,288,1152]{2,1,0:T(8,128)(2,1)} %w_out_ref.1, ...), custom_call_target="tpu_custom_call" | custom-call | flops 4000000000 | bytes 8000000 | tf_op jit(solution)/shard_map/pallas_call | solution.py:558
  49.7 1.6 %copy.9 = bf16[1,56,1152]{2,1,0:T(8,128)(2,1)} copy(bf16[1,56,1152]{2,1,0:T(8,128)(2,1)} %shard_map.73) | data formatting | bytes 258048

commit v7 on v6

--- a/solution.py
+++ b/solution.py
@@ -521,7 +521,7 @@
         sum_start(1, half)
     sum_across(1, n_part - 1)
     result = [finish(half) for half in range(n_part)]
-    out_ref[0] = jnp.concatenate(result, axis=0).astype(BF16)
+    out_ref[0] = jnp.concatenate(result, axis=0)
 
     for copy in pending:
         copy.wait_send()
@@ -557,7 +557,7 @@
     dma = pltpu.SemaphoreType.DMA
     return pl.pallas_call(
         functools.partial(kernel, n_tm, n_patch, width, wide, parts),
-        out_shape=jax.ShapeDtypeStruct(stream.shape, BF16),
+        out_shape=jax.ShapeDtypeStruct(stream.shape, F32),
         in_specs=[hbm] * 7,
         out_specs=vmem,
         scratch_shapes=[
@@ -595,7 +595,7 @@
         compiler_params=pltpu.CompilerParams(
             collective_id=0, has_side_effects=True, vmem_limit_bytes=56 * 1024 * 1024),
         cost_estimate=pl.CostEstimate(flops=4_000_000_000, bytes_accessed=8_000_000, transcendentals=1_000_000),
-    )(stream, stale_keys, stale_values, jnp.transpose(modulation, (1, 0, 2)), w_qkv, w_out, qk_gain)
+    )(stream, stale_keys, stale_values, jnp.transpose(modulation, (1, 0, 2)), w_qkv, w_out, qk_gain).astype(BF16)
 
 
 def solution(mesh):

time: 51.4 us -> 51.5 us (level)
  other arithmetic: 0 us -> 1.61 us
  local copies, waits for them, and re-layouts: 1.56 us -> 0 us
    convert_element_type x0 -> x1, other arithmetic: none -> 1.61 us  [local(): return pl.pallas_call(functools.partial(kernel, n_tm, n_patch, width, wid...]
    unnamed x1 -> x0, local copies, waits for them, and re-layouts: 1.56 us -> none
where the time goes in v7:
time: 51.5 us; the launch traced here: 51.4 us
  Pallas kernels  49.7 us (97%)
  other arithmetic  1.61 us (3%)
    pallas_call x1, Pallas kernels, local(): pl.pallas_call(functools.partial(kernel, n_tm, n_patch, width, wide, part...  49.7 us
    convert_element_type x1, other arithmetic, local(): return pl.pallas_call(functools.partial(kernel, n_tm, n_patch, width, wid...  1.61 us

profile of v7, /device:TPU:0, one launch (start us, length us, event | category | flops | bytes accessed | tf_op | source)
XLA Modules:
  0.0 51.4 jit_solution(7111806196228037838)
XLA Ops:
  0.0 49.7 %shard_map.73 = f32[1,56,1152]{2,1,0:T(8,128)} custom-call(bf16[1,56,1152]{2,1,0:T(8,128)(2,1)} %stream_ref.1, bf16[4,56,288]{2,1,0:T(8,128)(2,1)} %old_k_ref.1, bf16[4,56,288]{2,1,0:T(8,128)(2,1)} %old_v_ref.1, f32[3,2,1152]{2,1,0:T(2,128)} %bitcast.1, bf16[2,3,288,1152]{3,2,1,0:T(8,128)(2,1)} %w_qkv_ref.1, bf16[2,288,1152]{2,1,0:T(8,128)(2,1)} %w_out_ref.1, ...), custom_call_target="tpu_custom_call" | custom-call | flops 4000000000 | bytes 8000000 | tf_op jit(solution)/shard_map/pallas_call | solution.py:558
  49.7 1.6 %convert_element_type.3 = bf16[1,56,1152]{2,1,0:T(8,128)(2,1)} convert(f32[1,56,1152]{2,1,0:T(8,128)} %shard_map.73) | non-fusion elementwise | flops 64512 | bytes 387072 | tf_op jit(solution)/shard_map/convert_element_type | solution.py:598
